TPU v7x, 256 devices: a whole 4x4x8 slice. The times are simulated.
256 devices in a mesh: tile: 32 (over z, x), scan: 8 (over y, core).
Axes of the slice: x: 4, y: 4, z: 8, core: 2. Of those that a mesh axis runs over, the one named last changes fastest.
Arguments:
- object_field: float32 [2, 2, 512, 16384], P(None, None, None, 'tile'), may hold values from -1 to 1
- probe_wavefield: float32 [2, 2, 256, 256], replicated, may hold values from -3 to 3
- measured: float32 [32, 8, 2, 256, 256], P('tile', 'scan'), may hold values from 0 to 1
- offsets: int32 [32, 8, 2, 2], P('tile', 'scan'), may hold values from 0 to 511, as said below
- counts: int32 [32, 8], P('tile', 'scan'), may hold values from 0 to 2, as said below
Outputs:
- object_gradient: float32 [2, 2, 512, 16384], P(None, None, 'scan', 'tile')
- probe_gradient: float32 [2, 2, 256, 256], replicated
Inputs may be any that keep to these rules, and one draw needn't show every extreme that they name: `offsets`: offsets keep a window within the strip of its tile index and the next strip: row up to 256, column up to 511, and column up to 256 on the last tile index. The counts of the devices with one tile index sum to the number of scan groups.
All inputs are finite; a program needn't handle non-finite values.
Results may differ from a plain program's by a relative error of at most 0.0003.
Values sent between devices are 32-bit elements; how exact they have to be, the bound alone decides.
No kernel may reach another device: no remote copies, remote signals or barrier semaphores. Data moves between devices by JAX's collectives and lax.ppermute only.
A program may use at most 128 MiB of HBM per device.

v0:
```python
import math

import jax
import jax.numpy as jnp
from jax import lax
from jax.sharding import PartitionSpec as P


def shifted(shard, axis, by):
    peers = lax.axis_size(axis)
    pairs = [(i, i + by) for i in range(peers) if 0 <= i + by < peers]
    return lax.ppermute(shard, axis, pairs)


def precise_matmul(left_pair, right_pair):
    return jnp.matmul(left_pair, right_pair, precision=lax.Precision.HIGHEST)


def mat_product(left_pair, right_pair):
    real_part = precise_matmul(left_pair[0], right_pair[0]) - precise_matmul(
        left_pair[1], right_pair[1]
    )
    imag_part = precise_matmul(left_pair[0], right_pair[1]) + precise_matmul(
        left_pair[1], right_pair[0]
    )
    return (real_part, imag_part)


def transform(field_pair, table):
    return mat_product(table, mat_product(field_pair, table))


def complex_times(left_pair, right_pair):
    return (
        left_pair[0] * right_pair[0] - left_pair[1] * right_pair[1],
        left_pair[0] * right_pair[1] + left_pair[1] * right_pair[0],
    )


def times_conj(left_pair, right_pair):
    return (
        left_pair[0] * right_pair[0] + left_pair[1] * right_pair[1],
        left_pair[1] * right_pair[0] - left_pair[0] * right_pair[1],
    )


def make_tables(length):
    indices = jnp.arange(length, dtype=jnp.int32)
    phase_steps = indices[:, None] * indices[None, :] % length
    angles = 2.0 * math.pi / length * phase_steps.astype(jnp.float32)
    norm_scale = 1.0 / math.sqrt(length)
    forward_table = (jnp.cos(angles) * norm_scale, -jnp.sin(angles) * norm_scale)
    inverse_table = (forward_table[0], -forward_table[1])
    frequency = (indices + length // 2) % length - length // 2
    square = (frequency[:, None] * frequency[:, None] + frequency[None, :] * frequency[None, :]) % (
        4 * length
    )
    chirp_phase = 2.0 * math.pi / (4 * length) * square.astype(jnp.float32)
    transfer = (jnp.cos(chirp_phase), -jnp.sin(chirp_phase))
    return (forward_table, inverse_table, transfer)


def propagate(field_pair, lookup_tables):
    return transform(
        complex_times(transform(field_pair, lookup_tables[0]), lookup_tables[2]), lookup_tables[1]
    )


def back_propagate(field_pair, lookup_tables):
    return transform(
        times_conj(transform(field_pair, lookup_tables[0]), lookup_tables[2]), lookup_tables[1]
    )


def position_terms(window, probe_wavefield, measured_map, active_marker, lookup_tables):
    layers = window.shape[1]
    incoming = []
    field_now = (probe_wavefield[0], probe_wavefield[1])
    for depth_index in range(layers):
        if depth_index > 0:
            field_now = propagate(field_now, lookup_tables)
        incoming.append(field_now)
        field_now = complex_times(field_now, (window[0, depth_index], window[1, depth_index]))
    far_field = transform(field_now, lookup_tables[0])
    intensity = jnp.sum(far_field[0] * far_field[0] + far_field[1] * far_field[1], axis=0)
    misfit = (intensity - measured_map) * active_marker
    back_wave = transform((far_field[0] * misfit, far_field[1] * misfit), lookup_tables[1])
    layer_grads = []
    for depth_index in reversed(range(layers)):
        product_term = times_conj(back_wave, incoming[depth_index])
        layer_grads.append(
            jnp.stack([jnp.sum(product_term[0], axis=0), jnp.sum(product_term[1], axis=0)])
        )
        back_wave = times_conj(back_wave, (window[0, depth_index], window[1, depth_index]))
        if depth_index > 0:
            back_wave = back_propagate(back_wave, lookup_tables)
    patch_grad = jnp.stack(layer_grads[::-1], axis=1)
    return (patch_grad, jnp.stack([back_wave[0], back_wave[1]]))


def window_terms(
    padded_object, probe_wavefield, measured_map, offset_pair, active_marker, lookup_tables
):
    layers = padded_object.shape[1]
    window_size = probe_wavefield.shape[-1]
    zero_index = jnp.zeros((), jnp.int32)
    corner = (zero_index, zero_index, offset_pair[0], offset_pair[1])
    window = lax.dynamic_slice(padded_object, corner, (2, layers, window_size, window_size))
    return position_terms(window, probe_wavefield, measured_map, active_marker, lookup_tables)


def shards(object_field, probe_wavefield, measured, offsets, counts):
    window_size = probe_wavefield.shape[-1]
    strip_width = object_field.shape[3]
    layers = object_field.shape[1]
    slot_count = measured.shape[2]
    lookup_tables = make_tables(window_size)
    following = shifted(object_field[:, :, :, :window_size], "tile", -1)
    padded_object = jnp.concatenate([object_field, following], axis=3)
    local_measurements = measured[0, 0]
    local_scan_offsets = offsets[0, 0]
    own_count = counts[0, 0]
    task_list = []
    for position_index in range(slot_count):
        active_marker = (position_index < own_count).astype(jnp.float32)
        task_list.append(
            (local_measurements[position_index], local_scan_offsets[position_index], active_marker)
        )
    probe_total = jnp.zeros(probe_wavefield.shape, jnp.float32)
    results = []
    for task_measurements, task_scan_offsets, active_marker in task_list:
        patch_grad, probe_part = window_terms(
            padded_object,
            probe_wavefield,
            task_measurements,
            task_scan_offsets,
            active_marker,
            lookup_tables,
        )
        probe_total = probe_total + probe_part
        results.append((patch_grad, task_scan_offsets))
    zero_index = jnp.zeros((), jnp.int32)
    grad_ext = jnp.zeros(padded_object.shape, jnp.float32)
    for patch_grad, task_scan_offsets in results:
        corner = (zero_index, zero_index, task_scan_offsets[0], task_scan_offsets[1])
        current = lax.dynamic_slice(grad_ext, corner, (2, layers, window_size, window_size))
        grad_ext = lax.dynamic_update_slice(grad_ext, current + patch_grad, corner)
    strip_grad = grad_ext[:, :, :, :strip_width]
    edge_grad = grad_ext[:, :, :, strip_width:]
    incoming_edge = shifted(edge_grad, "tile", 1)
    combined = jnp.concatenate(
        [strip_grad[:, :, :, :window_size] + incoming_edge, strip_grad[:, :, :, window_size:]],
        axis=3,
    )
    result = lax.psum_scatter(combined, "scan", scatter_dimension=2, tiled=True)
    probe_sum = lax.psum(probe_total, ("tile", "scan"))
    probe_result = probe_sum / math.sqrt(lax.axis_size("tile") * lax.axis_size("scan"))
    return (result, probe_result)


def solution(mesh):
    in_specs = (
        P(None, None, None, "tile"),
        P(),
        P("tile", "scan", None, None, None),
        P("tile", "scan", None, None),
        P("tile", "scan"),
    )
    out_specs = (P(None, None, "scan", "tile"), P())
    return jax.shard_map(shards, mesh=mesh, in_specs=in_specs, out_specs=out_specs, check_vma=False)
```

profile of v0, /device:TPU:2, one launch (start us, length us, event | category | flops | bytes accessed | tf_op | source)
XLA Modules:
  0.0 534.3 jit_solution(15494000162756647113)
XLA Ops:
  8.1 3.1 slice.92
  11.1 4.2 collective-permute-start
  24.0 2.6 constant_dynamic-update-slice_fusion.1
  27.7 32.9 %collective-permute-done = f32[2,2,512,256]{3,2,1,0:T(8,128)S(1)} collective-permute-done((f32[2,2,512,256]{3,2,1,0:T(8,128)}, f32[2,2,512,256]{3,2,1,0:T(8,128)S(1)}, u32[]{:S(2)}, u32[]{:S(2)}) %collective-permute-start) | collective-permute-done | bytes 2097184 | tf_op jit(solution)/shard_map/ppermute | solution.py:12
  69.5 2.0 fusion.175
  82.8 1.8 fusion.169
  94.3 1.8 convolution_add_fusion.23
  107.5 2.0 convolution_add_fusion.21
  119.3 1.8 fusion.56
  130.8 1.8 fusion.197
  139.3 1.7 add_reduce_fusion.3
  144.3 2.0 convolution_add_fusion.5
  152.8 2.5 add_reduce_fusion
  156.9 1.8 fusion.14
  170.1 1.8 fusion.8
  181.5 2.0 convolution_subtract_fusion.16
  183.6 1.8 add_reduce_fusion.2
  193.5 1.8 fusion.188
  206.6 1.8 fusion.145
  218.2 1.9 fusion.2
  220.1 4.0 add_bitcast_fusion
  224.3 3.2 broadcast_in_dim.2
  227.5 10.8 %dynamic_update_slice.6 = f32[2,2,512,768]{3,2,1,0:T(8,128)} dynamic-update-slice(f32[2,2,512,768]{3,2,1,0:T(8,128)} %broadcast_in_dim.2, f32[2,2,256,256]{3,2,1,0:T(8,128)S(1)} %pad_maximum_fusion.1, s32[]{:T(128)} %constant.47.clone.1, s32[]{:T(128)} %constant.47.clone.1, s32[]{:T(128)S(6)} %select_n.301, s32[]{:T(128)S(6)} %select_n.302) | dynamic-update-slice | bytes 2097156 | tf_op jit(solution)/shard_map/dynamic_update_slice | solution.py:147
  239.4 1.9 maximum_add_fusion
  241.3 12.0 %dynamic_update_slice.7 = f32[2,2,512,768]{3,2,1,0:T(8,128)} dynamic-update-slice(f32[2,2,512,768]{3,2,1,0:T(8,128)} %dynamic_update_slice.6, f32[2,2,256,256]{3,2,1,0:T(8,128)S(1)} %maximum_add_fusion, s32[]{:T(128)} %constant.47.clone.1, s32[]{:T(128)} %constant.47.clone.1, s32[]{:T(128)S(6)} %select_n.305, s32[]{:T(128)S(6)} %select_n.306) | dynamic-update-slice | bytes 2097156 | tf_op jit(solution)/shard_map/dynamic_update_slice | solution.py:147
  253.3 3.1 slice.112
  256.4 4.0 collective-permute-start.1
  261.7 45.2 %collective-permute-done.1 = f32[2,2,512,256]{3,2,1,0:T(8,128)} collective-permute-done((f32[2,2,512,256]{3,2,1,0:T(8,128)}, f32[2,2,512,256]{3,2,1,0:T(8,128)}, u32[]{:S(2)}, u32[]{:S(2)}) %collective-permute-start.1) | collective-permute-done | bytes 2097184 | tf_op jit(solution)/shard_map/ppermute | solution.py:12
  306.9 3.3 slice_add_fusion
  310.2 2.5 pad_maximum_fusion
  312.7 211.5 %all-reduce.2.cloned.1.call-done = f32[2,2,256,256]{3,2,1,0:T(8,128)} async-done(((f32[2,2,256,256]{3,2,1,0:T(8,128)}), f32[2,2,256,256]{3,2,1,0:T(8,128)}) %all-reduce.2.cloned.1.call-update) | async-done | bytes 1048592 | tf_op jit(solution)/shard_map/psum | solution.py:156
  524.2 2.3 broadcast_multiply_fusion
  (106 shorter events, 132.5 us)
Async XLA Ops:
  8.0 7.3 %copy-start.5 = (s32[1,1,2,2]{3,2,1,0:T(2,128)S(1)}, s32[1,1,2,2]{3,2,1,0:T(2,128)}, u32[]{:S(2)}) copy-start(s32[1,1,2,2]{3,2,1,0:T(2,128)} %param.8) | copy-start | bytes 52
  8.0 516.2 %all-reduce.2.cloned.1.call-start = ((), (), s32[]{:S(2)}) async-start(), calls=%async_computation.2 | async-start | bytes 2097152 | tf_op jit(solution)/shard_map/psum | solution.py:156
  11.1 49.5 %collective-permute-start = (f32[2,2,512,256]{3,2,1,0:T(8,128)}, f32[2,2,512,256]{3,2,1,0:T(8,128)S(1)}, u32[]{:S(2)}, u32[]{:S(2)}) collective-permute-start(f32[2,2,512,256]{3,2,1,0:T(8,128)} %slice.92), channel_id=1, source_target_pairs={{8,0},{16,8},{24,16},{32,24},{40,32},{48,40},{56,48},{64,56},{72,6... | collective-permute-start | bytes 6291464 | tf_op jit(solution)/shard_map/ppermute | solution.py:12
  27.7 33.7 %copy-start = (f32[2,2,256,256]{3,2,1,0:T(8,128)S(1)}, f32[2,2,256,256]{3,2,1,0:T(8,128)}, u32[]{:S(2)}) copy-start(f32[2,2,256,256]{3,2,1,0:T(8,128)} %param.6) | copy-start | bytes 3145732
  134.3 6.8 %copy-start.4 = (f32[1,1,2,256,256]{4,3,2,1,0:T(8,128)S(1)}, f32[1,1,2,256,256]{4,3,2,1,0:T(8,128)}, u32[]{:S(2)}) copy-start(f32[1,1,2,256,256]{4,3,2,1,0:T(8,128)} %param.7) | copy-start | bytes 1572868
  224.3 14.1 %copy-start.2 = (f32[256,256]{1,0:T(8,128)S(1)}, f32[256,256]{1,0:T(8,128)}, u32[]{:S(2)}) copy-start(f32[256,256]{1,0:T(8,128)} %get-tuple-element.5) | copy-start | bytes 786436
  224.3 14.0 %copy-start.3 = (f32[256,256]{1,0:T(8,128)S(1)}, f32[256,256]{1,0:T(8,128)}, u32[]{:S(2)}) copy-start(f32[256,256]{1,0:T(8,128)} %get-tuple-element.28) | copy-start | bytes 786436
  239.4 21.1 %copy-start.1 = (f32[1,2,256,256]{3,2,1,0:T(8,128)S(1)}, f32[1,2,256,256]{3,2,1,0:T(8,128)}, u32[]{:S(2)}) copy-start(f32[1,2,256,256]{3,2,1,0:T(8,128)} %get-tuple-element.31) | copy-start | bytes 1572868
  256.4 50.5 %collective-permute-start.1 = (f32[2,2,512,256]{3,2,1,0:T(8,128)}, f32[2,2,512,256]{3,2,1,0:T(8,128)}, u32[]{:S(2)}, u32[]{:S(2)}) collective-permute-start(f32[2,2,512,256]{3,2,1,0:T(8,128)} %slice.112), channel_id=1, source_target_pairs={{0,8},{8,16},{16,24},{24,32},{32,40},{40,48},{48,56},{56,64},{64,7... | collective-permute-start | bytes 6291464 | tf_op jit(solution)/shard_map/ppermute | solution.py:12
  261.6 264.8 %reduce-scatter.2.cloned.1.call-start = ((), (), s32[]{:S(2)}) async-start(), calls=%async_computation.1 | async-start | bytes 4718592 | tf_op jit(solution)/shard_map/reduce_scatter | solution.py:155
Sparse Core Ops, SparseCore 0:
  261.7 262.3 all-reduce.1
Sparse Core Ops, SparseCore 1:
  312.8 46.3 reduce-scatter.1
where the time goes:
time: 544 us; the launch traced here: 534 us
  waiting for transfers between devices  290 us (53%)
  matrix products  162 us (30%)
  local copies, waits for them, and re-layouts  36.3 us (7%)
  between operations  24.9 us (5%)
  other arithmetic  13.4 us (2%)
  starting transfers between devices  8.29 us (2%)
    psum x1, waiting for transfers between devices, shards(): probe_sum = lax.psum(probe_total, ('tile', 'scan'))  211 us
    dot_general x96, matrix products, precise_matmul(): return jnp.matmul(left_pair, right_pair, precision=lax.Precision.HIGHEST)  162 us
    ppermute x2, waiting for transfers between devices, shifted(): return lax.ppermute(shard, axis, pairs)  78.1 us
    dynamic_update_slice x2, local copies, waits for them, and re-layouts, shards(): grad_ext = lax.dynamic_update_slice(grad_ext, current + patch_grad, corner)  22.8 us
  transfers between devices with their start and end apart: 4, of which 3 were waited for; matrix products, arithmetic and copies ran while one was open for 3% of the time, Pallas kernels for 0%

commit v1 on v0

v1 whole, which is shorter than its diff:
```python
import math

import jax
import jax.numpy as jnp
import ml_dtypes
import numpy as np
from jax import lax
from jax.experimental import pallas as pl
from jax.experimental.pallas import tpu as pltpu
from jax.sharding import PartitionSpec as P

BF = jnp.bfloat16
F32 = jnp.float32
VMEM_BYTES = 40 << 20


def split_table(table):
    high = table.astype(ml_dtypes.bfloat16)
    low = (table - high.astype(np.float64)).astype(ml_dtypes.bfloat16)
    return high, low


def make_tables(n):
    j = np.arange(n)
    phase = 2 * np.pi * ((j[:, None] * j[None, :]) % n) / n
    cas = (np.cos(phase) + np.sin(phase)) / math.sqrt(n)
    sigma = np.concatenate([np.arange(n // 2), [n // 2], np.arange(n - 1, n // 2, -1)])
    high, low = split_table(cas)
    phigh, plow = split_table(cas[sigma])
    left = np.concatenate([high, high, low], 1)
    right = np.concatenate([high, high, low], 0)
    left_in = np.concatenate([phigh, phigh, plow], 1)
    right_in = np.concatenate([phigh.T, phigh.T, plow.T], 0)
    left_out = np.concatenate([phigh.T, phigh.T, plow.T], 1)
    right_out = np.concatenate([phigh, phigh, plow], 0)
    f = (j + n // 2) % n - n // 2
    q = (f[:, None] ** 2 + f[None, :] ** 2) % (4 * n)
    chirp = 2 * np.pi * q / (4 * n)
    transfer = np.stack([np.cos(chirp), -np.sin(chirp)]).astype(np.float32)
    perm = np.zeros((n, n))
    perm[j, sigma] = 1
    return {
        "plain": (left, right),
        "far": (left_in, right_in),
        "back": (left_out, right_out),
        "transfer": transfer,
        "perm": perm.astype(ml_dtypes.bfloat16),
    }


def split(x):
    high = x.astype(BF)
    return high, (x - high.astype(F32)).astype(BF)


def dot(a, b):
    return jnp.dot(a, b, preferred_element_type=F32)


def right_mul(x, table):
    high, low = split(x)
    return dot(jnp.concatenate([high, low, high], 1), table)


def left_mul(table, x):
    high, low = split(x)
    return dot(table, jnp.concatenate([high, low, high], 0))


def two_sided(pair, tables):
    return tuple(left_mul(tables[0][...], right_mul(p, tables[1][...])) for p in pair)


def cmul(a, b):
    return a[0] * b[0] - a[1] * b[1], a[0] * b[1] + a[1] * b[0]


def cmulc(a, b):
    return a[0] * b[0] + a[1] * b[1], a[1] * b[0] - a[0] * b[1]


def swap_rows(z):
    n = z.shape[0]
    h = n // 2
    fixed = lax.broadcasted_iota(jnp.int32, z.shape, 0) % h == 0
    return jnp.where(fixed, z, jnp.concatenate([z[h:], z[:h]], 0))


def swap_cols(z):
    n = z.shape[1]
    h = n // 2
    fixed = lax.broadcasted_iota(jnp.int32, z.shape, 1) % h == 0
    return jnp.where(fixed, z, jnp.concatenate([z[:, h:], z[:, :h]], 1))


def mix(pair, sign):
    a, b = pair
    ca, cb = swap_cols(a), swap_cols(b)
    re = 0.5 * (sign * (b - swap_rows(cb)) + (swap_rows(a) + ca))
    im = 0.5 * (sign * (swap_rows(ca) - a) + (swap_rows(b) + cb))
    return re, im


def corner_of(offs, slot, rows):
    r, c = offs[2 * slot], offs[2 * slot + 1]
    row = jnp.minimum(lax.div(r, 8), rows // 8 - 33) * 8
    col = lax.div(c, 128) * 128
    return pl.multiple_of(row, 8), pl.multiple_of(col, 128), r - row, c - col


def take_window(ext, offs, slot, part):
    row, col, dr, dc = corner_of(offs, slot, ext.shape[1])
    x = ext[part, pl.ds(row, 264), pl.ds(col, 384)]
    x = pltpu.roll(x, lax.rem(384 - dc, 384), 1)
    x = pltpu.roll(x, lax.rem(264 - dr, 264), 0)
    return x[:256, :256]


def add_window(acc, offs, slot, part, g):
    row, col, dr, dc = corner_of(offs, slot, acc.shape[1])
    x = jnp.pad(g, ((0, 8), (0, 128)))
    x = pltpu.roll(x, dc, 1)
    x = pltpu.roll(x, dr, 0)
    acc[part, pl.ds(row, 264), pl.ds(col, 384)] += x


def load_ext(strip, layer, pieces, offs, ext, sem):
    copy = pltpu.make_async_copy(strip.at[:, layer], ext.at[:, :, pl.ds(0, 512)], sem)
    copy.start()
    y, c = offs[4], offs[5]
    half = lax.rem(y, 2)
    for k, piece in enumerate(pieces):
        hh = half if k % 2 == 0 else 1 - half
        cc = c if k < 2 else 1 - c
        row = pl.multiple_of(256 * hh + 128 * cc, 128)
        ext[:, pl.ds(row, 128), pl.ds(512, 256)] = piece[...]
    copy.wait()


def propagate_kernel(offs, strip, h0, h1, h2, h3, probe, tl, tr, transfer, o1, u, ext, sem):
    load_ext(strip, 0, (h0, h1, h2, h3), offs, ext, sem)

    @pl.loop(0, 2)
    def _(slot):
        @pl.when(slot < offs[6])
        def _():
            for part in range(2):
                o1[slot, part] = take_window(ext, offs, slot, part)
            obj = (o1[slot, 0], o1[slot, 1])
            h = (transfer[0], transfer[1])
            for m in range(2):
                w = cmul((probe[0, m], probe[1, m]), obj)
                z = cmul(two_sided(w, (tl, tr)), h)
                g = two_sided(z, (tl, tr))
                u[slot, m, 0] = g[0]
                u[slot, m, 1] = g[1]


def write_blocks(acc, offs, keep, send, keep_sib, send_sib):
    y, c = offs[4], offs[5]
    a, b = jnp.bitwise_xor(y, 1), 3 - y
    p = jnp.where(c == 0, a, b)
    o = jnp.where(c == 0, b, a)
    q = 3 - a

    def block(chip, core):
        row = pl.multiple_of(128 * chip + 64 * core, 64)
        return acc[:, pl.ds(row, 64), :]

    send_sib[0] = block(o, 1 - c)
    send_sib[1] = block(q, 1 - c)
    send[0] = block(p, c)
    send[1] = block(q, c)
    keep_sib[0] = block(y, 1 - c)
    keep_sib[1] = block(p, 1 - c)
    keep[0] = block(y, c)
    keep[1] = block(o, c)


def far_kernel(
    offs, strip, h0, h1, h2, h3, u, meas, perm, fl, fr, bl, br,
    c2, keep, send, keep_sib, send_sib, ext, acc, psi, sem,
):
    load_ext(strip, 1, (h0, h1, h2, h3), offs, ext, sem)
    acc[...] = jnp.zeros_like(acc)

    @pl.loop(0, 2)
    def _(slot):
        @pl.when(slot < offs[6])
        def _():
            obj = tuple(take_window(ext, offs, slot, part) for part in range(2))
            pm = perm[...]
            high, low = split(meas[slot])
            high, low = split(dot(pm, high) + dot(pm, low))
            dims = (((1,), (1,)), ((), ()))
            misfit = -(
                lax.dot_general(high, pm, dims, preferred_element_type=F32)
                + lax.dot_general(low, pm, dims, preferred_element_type=F32)
            )
            for m in range(2):
                w = cmul((u[slot, m, 0], u[slot, m, 1]), obj)
                re, im = mix(two_sided(w, (fl, fr)), 1.0)
                psi[m, 0] = re
                psi[m, 1] = im
                misfit = misfit + (re * re + im * im)
            total = None
            for m in range(2):
                v = mix((psi[m, 0] * misfit, psi[m, 1] * misfit), -1.0)
                g = two_sided(v, (bl, br))
                term = cmulc(g, (u[slot, m, 0], u[slot, m, 1]))
                total = term if total is None else (total[0] + term[0], total[1] + term[1])
                c = cmulc(g, obj)
                c2[slot, m, 0] = c[0]
                c2[slot, m, 1] = c[1]
            for part in range(2):
                add_window(acc, offs, slot, part, total[part])

    write_blocks(acc, offs, keep, send, keep_sib, send_sib)


def back_kernel(
    offs, c2, o1, probe, tl, tr, transfer,
    mine, sib, keep, send, keep_sib, send_sib, acc, pacc,
):
    acc[...] = jnp.zeros_like(acc)
    pacc[...] = jnp.zeros_like(pacc)

    @pl.loop(0, 2)
    def _(slot):
        @pl.when(slot < offs[6])
        def _():
            obj = (o1[slot, 0], o1[slot, 1])
            h = (transfer[0], transfer[1])
            total = None
            for m in range(2):
                z = cmulc(two_sided((c2[slot, m, 0], c2[slot, m, 1]), (tl, tr)), h)
                g = two_sided(z, (tl, tr))
                term = cmulc(g, (probe[0, m], probe[1, m]))
                total = term if total is None else (total[0] + term[0], total[1] + term[1])
                c = cmulc(g, obj)
                pacc[m, 0] += c[0]
                pacc[m, 1] += c[1]
            for part in range(2):
                add_window(acc, offs, slot, part, total[part])

    c = offs[5]
    mine[...] = pacc[c]
    sib[...] = pacc[1 - c]
    write_blocks(acc, offs, keep, send, keep_sib, send_sib)


def struct(*shape):
    return jax.ShapeDtypeStruct(shape, F32)


def run_kernel(body, name, ins, outs, scratch, flops, n_any=()):
    specs = []
    for i in range(len(ins)):
        if i == 0:
            specs.append(pl.BlockSpec(memory_space=pltpu.SMEM))
        elif i in n_any:
            specs.append(pl.BlockSpec(memory_space=pl.ANY))
        else:
            specs.append(pl.BlockSpec(memory_space=pltpu.VMEM))
    return pl.pallas_call(
        body,
        out_shape=outs,
        in_specs=specs,
        out_specs=[pl.BlockSpec(memory_space=pltpu.VMEM)] * len(outs),
        scratch_shapes=scratch,
        compiler_params=pltpu.CompilerParams(vmem_limit_bytes=VMEM_BYTES),
        cost_estimate=pl.CostEstimate(flops=flops, bytes_accessed=8 << 20, transcendentals=0),
        name=name,
    )(*ins)


def pairs(n, f):
    return [(i, f(i)) for i in range(n)]


def core_swap(x):
    return lax.ppermute(x, "c", [(0, 1), (1, 0)])


def pattern(first):
    def f(i):
        y, c = i // 2, i % 2
        return 2 * ((y ^ 1) if (c == 0) == first else 3 - y) + c

    return pairs(8, f)


def y_swap(x, first):
    return lax.ppermute(x, ("y", "c"), pattern(first))


def tile_shift(x, by):
    n = lax.axis_size("z") * lax.axis_size("x")
    return lax.ppermute(x, ("z", "x"), [(i, i + by) for i in range(n) if 0 <= i + by < n])


def reduce_rows(keep, send, keep_sib, send_sib):
    got_send = core_swap(send_sib)
    got_keep = core_swap(keep_sib)
    got = y_swap(send + got_send, True)
    kept = keep + got_keep + got
    return kept[0] + y_swap(kept[1], False)


def finish(rows):
    edge = tile_shift(rows[:, :, 512:], 1)
    return jnp.concatenate([rows[:, :, :256] + edge, rows[:, :, 256:512]], 2)


def shards(object_field, probe, measured, offsets, counts):
    n = probe.shape[-1]
    tables = make_tables(n)
    y, c = lax.axis_index("y"), lax.axis_index("c")
    offs = jnp.concatenate(
        [offsets.reshape(4), y.astype(jnp.int32)[None], c.astype(jnp.int32)[None], counts.reshape(1)]
    )
    zero = jnp.zeros((), jnp.int32)
    row = (256 * lax.rem(y, 2) + 128 * c).astype(jnp.int32)
    halos = []
    for layer in range(2):
        part = lax.dynamic_slice(object_field[:, layer], (zero, row, zero), (2, 128, n))
        halos.append(tile_shift(part, -1))
    pieces = []
    for got in halos:
        other = y_swap(got, True)
        pieces.append((got, other, core_swap(got), core_swap(other)))

    tl, tr = (jnp.asarray(t) for t in tables["plain"])
    fl, fr = (jnp.asarray(t) for t in tables["far"])
    bl, br = (jnp.asarray(t) for t in tables["back"])
    transfer = jnp.asarray(tables["transfer"])
    perm = jnp.asarray(tables["perm"])
    meas = measured[0, 0]
    ext = pltpu.VMEM((2, 512, 768), F32)
    sem = pltpu.SemaphoreType.DMA(())
    blocks = [struct(2, 2, 64, 768)] * 4
    flops = 16 * 3 * 2 * n**3
    o1, u = run_kernel(
        propagate_kernel, "propagate",
        (offs, object_field, *pieces[0], probe, tl, tr, transfer),
        [struct(2, 2, n, n), struct(2, 2, 2, n, n)],
        [ext, sem], 2 * flops, n_any=(1,),
    )
    c2, *far_blocks = run_kernel(
        far_kernel, "far_field",
        (offs, object_field, *pieces[1], u, meas, perm, fl, fr, bl, br),
        [struct(2, 2, 2, n, n)] + blocks,
        [ext, pltpu.VMEM((2, 512, 768), F32), pltpu.VMEM((2, 2, n, n), F32), sem],
        2 * flops, n_any=(1,),
    )
    mine, sib, *near_blocks = run_kernel(
        back_kernel, "back",
        (offs, c2, o1, probe, tl, tr, transfer),
        [struct(2, n, n), struct(2, n, n)] + blocks,
        [pltpu.VMEM((2, 512, 768), F32), pltpu.VMEM((2, 2, n, n), F32)],
        2 * flops,
    )

    total = (mine + core_swap(sib)).reshape(16, 64, 128)
    total = jnp.sum(lax.all_to_all(total, ("x", "y"), 0, 0, tiled=True), axis=0)
    total = jnp.broadcast_to(total, (8, 64, 128))
    total = jnp.sum(lax.all_to_all(total, "z", 0, 0, tiled=True), axis=0) * (1.0 / 16.0)
    total = jnp.broadcast_to(total, (16, 64, 128))
    total = lax.all_to_all(total, ("x", "y"), 0, 0, tiled=True).reshape(2, n, n)
    other = core_swap(total)
    first = jnp.where(c == 0, total, other)
    second = jnp.where(c == 0, other, total)
    probe_gradient = jnp.stack([first, second], axis=1)

    far_rows = finish(reduce_rows(*far_blocks))
    near_rows = finish(reduce_rows(*near_blocks))
    return jnp.stack([near_rows, far_rows], axis=1), probe_gradient


def solution(mesh):
    sizes = (8, 4, 4, 2)
    split_mesh = jax.sharding.Mesh(mesh.devices.reshape(sizes), ("z", "x", "y", "c"))
    tile, scan = ("z", "x"), ("y", "c")
    in_specs = (
        P(None, None, None, tile),
        P(),
        P(tile, scan, None, None, None),
        P(tile, scan, None, None),
        P(tile, scan),
    )
    out_specs = (P(None, None, scan, tile), P())
    return jax.shard_map(
        shards, mesh=split_mesh, in_specs=in_specs, out_specs=out_specs, check_vma=False
    )
```

time: 544 us -> 146 us (0.27)
  the two profiles are of different devices: /device:TPU:2 before, /device:TPU:32 now
where the time goes in v1:
time: 146 us; the launch traced here: 144 us
  starting transfers between devices  55.8 us (38%)
  waiting for transfers between devices  39.5 us (27%)
  local copies, waits for them, and re-layouts  18.3 us (13%)
  Pallas kernels  17.6 us (12%)
  other arithmetic  11.4 us (8%)
  between operations  1.73 us (1%)
    all_to_all x1, starting transfers between devices, shards(): total = jnp.sum(lax.all_to_all(total, ('x', 'y'), 0, 0, tiled=True), axis=0)  20.1 us
    pallas_call x3, Pallas kernels, run_kernel(): pl.pallas_call(body, out_shape=outs, in_specs=specs, out_specs=[pl.BlockS...  17.6 us
    ppermute x4, starting transfers between devices, tile_shift(): lax.ppermute(x, ('z', 'x'), [(i, i + by) for i in range(n) if 0 <= i + by...  12.7 us
    ppermute x6, waiting for transfers between devices, y_swap(): return lax.ppermute(x, ('y', 'c'), pattern(first))  11.3 us
    ppermute x4, waiting for transfers between devices, tile_shift(): lax.ppermute(x, ('z', 'x'), [(i, i + by) for i in range(n) if 0 <= i + by...  9.65 us
    all_to_all x1, starting transfers between devices, shards(): lax.all_to_all(total, 'z', 0, 0, tiled=True)  8.78 us
    unnamed x41, local copies, waits for them, and re-layouts  7.88 us
    all_to_all x1, waiting for transfers between devices, shards(): total = jnp.sum(lax.all_to_all(total, ('x', 'y'), 0, 0, tiled=True), axis=0)  7.84 us
  transfers between devices with their start and end apart: 23, of which 10 were waited for; matrix products, arithmetic and copies ran while one was open for 11% of the time, Pallas kernels for 7%

profile of v1, /device:TPU:32, one launch (start us, length us, event | category | flops | bytes accessed | tf_op | source)
XLA Modules:
  0.0 144.4 jit_solution(16806788544012737884)
XLA Ops:
  0.7 4.8 %fusion.2 = (f32[2,1,512,512]{3,2,1,0:T(8,128)}, f32[2,1,512,512]{3,2,1,0:T(8,128)}) fusion(f32[2,2,512,512]{3,2,1,0:T(8,128)} %strip.3), kind=kLoop, calls=%fused_computation.20 | loop fusion | bytes 8388608 | tf_op jit(solution)/shard_map/slice | solution.py:326
  6.4 4.2 %collective-permute-start.4 = (f32[2,128,256]{2,1,0:T(8,128)S(1)}, f32[2,128,256]{2,1,0:T(8,128)S(1)}, u32[]{:S(2)}, u32[]{:S(2)}) collective-permute-start(f32[2,128,256]{2,1,0:T(8,128)S(1)} %dynamic-slice_bitcast_fusion), channel_id=1, source_target_pairs={{8,0},{16,8},{24,16},{32,24},{40,32},{48,40},{56,48},{64,56},{72,6... | collective-permute-start | bytes 786440 | tf_op jit(solution)/shard_map/ppermute | solution.py:299
  11.6 2.7 %collective-permute-start = (f32[2,128,256]{2,1,0:T(8,128)S(1)}, f32[2,128,256]{2,1,0:T(8,128)S(1)}, u32[]{:S(2)}, u32[]{:S(2)}) collective-permute-start(f32[2,128,256]{2,1,0:T(8,128)S(1)} %dynamic-slice_bitcast_fusion.1), channel_id=1, source_target_pairs={{8,0},{16,8},{24,16},{32,24},{40,32},{48,40},{56,48},{64,56},{72,6... | collective-permute-start | bytes 786440 | tf_op jit(solution)/shard_map/ppermute | solution.py:299
  14.4 3.0 %collective-permute-done.4.h0 = f32[2,128,256]{2,1,0:T(8,128)S(1)} collective-permute-done((f32[2,128,256]{2,1,0:T(8,128)S(1)}, f32[2,128,256]{2,1,0:T(8,128)S(1)}, u32[]{:S(2)}, u32[]{:S(2)}) %collective-permute-start.4) | collective-permute-done | bytes 262176 | tf_op jit(solution)/shard_map/ppermute | solution.py:299
  17.3 1.6 %collective-permute-start.5 = (f32[2,128,256]{2,1,0:T(8,128)S(1)}, f32[2,128,256]{2,1,0:T(8,128)S(1)}, u32[]{:S(2)}, u32[]{:S(2)}) collective-permute-start(f32[2,128,256]{2,1,0:T(8,128)S(1)} %collective-permute-done.4.h0), channel_id=1, source_target_pairs={{0,2},{1,7},{2,0},{3,5},{4,6},{5,3},{6,4},{7,1},{8,10},{9,15},{10,... | collective-permute-start | bytes 786440 | tf_op jit(solution)/shard_map/ppermute | solution.py:294
  18.9 3.1 %collective-permute-done.h0 = f32[2,128,256]{2,1,0:T(8,128)S(1)} collective-permute-done((f32[2,128,256]{2,1,0:T(8,128)S(1)}, f32[2,128,256]{2,1,0:T(8,128)S(1)}, u32[]{:S(2)}, u32[]{:S(2)}) %collective-permute-start) | collective-permute-done | bytes 262176 | tf_op jit(solution)/shard_map/ppermute | solution.py:299
  22.0 1.6 %collective-permute-start.1 = (f32[2,128,256]{2,1,0:T(8,128)S(1)}, f32[2,128,256]{2,1,0:T(8,128)S(1)}, u32[]{:S(2)}, u32[]{:S(2)}) collective-permute-start(f32[2,128,256]{2,1,0:T(8,128)S(1)} %collective-permute-done.h0), channel_id=1, source_target_pairs={{0,2},{1,7},{2,0},{3,5},{4,6},{5,3},{6,4},{7,1},{8,10},{9,15},{10,... | collective-permute-start | bytes 786440 | tf_op jit(solution)/shard_map/ppermute | solution.py:294
  25.4 2.9 %collective-permute-done.1.h1 = f32[2,128,256]{2,1,0:T(8,128)S(1)} collective-permute-done((f32[2,128,256]{2,1,0:T(8,128)S(1)}, f32[2,128,256]{2,1,0:T(8,128)S(1)}, u32[]{:S(2)}, u32[]{:S(2)}) %collective-permute-start.1) | collective-permute-done | bytes 262176 | tf_op jit(solution)/shard_map/ppermute | solution.py:294
  28.4 2.2 %copy-done = f32[2,2,512,512]{3,2,1,0:T(8,128)S(1)} copy-done((f32[2,2,512,512]{3,2,1,0:T(8,128)S(1)}, f32[2,2,512,512]{3,2,1,0:T(8,128)}, u32[]{:S(2)}) %copy-start) | copy-done | bytes 4194328
  32.7 4.4 %propagate.1 = (f32[2,2,256,256]{3,2,1,0:T(8,128)S(1)}, f32[2,2,2,256,256]{4,3,2,1,0:T(8,128)S(1)}) custom-call(s32[7]{0:T(128)S(1)} %pad_add_fusion.offs, f32[2,2,512,512]{3,2,1,0:T(8,128)S(1)} %copy-done, f32[2,128,256]{2,1,0:T(8,128)S(1)} %collective-permute-done.4.h0, f32[2,128,256]{2,1,0:T(8,128)S(1)} %collective-permute-done.5.h1, ...), custom_call_target="tpu_custom_call" | custom-call | flops 3221225472 | bytes 8388608 | tf_op jit(solution)/shard_map/propagate/pallas_call | solution.py:265
  38.1 7.7 %far_field.1 = (f32[2,2,2,256,256]{4,3,2,1,0:T(8,128)S(1)}, f32[2,2,64,768]{3,2,1,0:T(8,128)S(1)}, f32[2,2,64,768]{3,2,1,0:T(8,128)S(1)}, f32[2,2,64,768]{3,2,1,0:T(8,128)S(1)}, f32[2,2,64,768]{3,2,1,0:T(8,128)}) custom-call(s32[7]{0:T(128)S(1)} %pad_add_fusion.offs, f32[2,2,512,512]{3,2,1,0:T(8,128)} %strip.3, f32[2,128,256]{2,1,0:T(8,128)S(1)} %collective-permute-done.h0, ...), custom_call_target="tpu_custom_call" | custom-call | flops 3221225472 | bytes 8388608 | tf_op jit(solution)/shard_map/far_field/pallas_call | solution.py:265
  47.1 5.6 %back.1 = (f32[2,256,256]{2,1,0:T(8,128)S(1)}, f32[2,256,256]{2,1,0:T(8,128)S(1)}, f32[2,2,64,768]{3,2,1,0:T(8,128)S(1)}, f32[2,2,64,768]{3,2,1,0:T(8,128)S(1)},...) custom-call(s32[7]{0:T(128)S(1)} %pad_add_fusion.offs, f32[2,2,2,256,256]{4,3,2,1,0:T(8,128)S(1)} %get-tuple-element.16.c2, ...), custom_call_target="tpu_custom_call" | custom-call | flops 3221225472 | bytes 8388608 | tf_op jit(solution)/shard_map/back/pallas_call | solution.py:265
  54.1 1.4 collective-permute-done.18
  56.4 1.9 %reshape.20 = f32[16,64,128]{2,1,0:T(8,128)} reshape(f32[2,256,256]{2,1,0:T(8,128)} %add.52) | data formatting | bytes 1048576 | tf_op jit(solution)/shard_map/reshape | solution.py:364
  58.3 20.1 %all-to-all-start = ((f32[16,64,128]{2,1,0:T(8,128)}), f32[16,64,128]{2,1,0:T(8,128)}, u32[]{:S(2)}, u32[]{:S(2)}) async-start(f32[16,64,128]{2,1,0:T(8,128)} %reshape.20), calls=%async_computation | async-start | bytes 1048576 | tf_op jit(solution)/shard_map/all_to_all | solution.py:365
  78.5 2.2 %add.48 = f32[2,2,64,768]{3,2,1,0:T(8,128)} add(f32[2,2,64,768]{3,2,1,0:T(8,128)S(1)} %get-tuple-element.24, f32[2,2,64,768]{3,2,1,0:T(8,128)} %collective-permute-done.14) | non-fusion elementwise | flops 196608 | bytes 2359296 | tf_op jit(solution)/shard_map/add | solution.py:305
  80.7 1.8 %collective-permute-start.15 = (f32[2,2,64,768]{3,2,1,0:T(8,128)}, f32[2,2,64,768]{3,2,1,0:T(8,128)S(1)}, u32[]{:S(2)}, u32[]{:S(2)}) collective-permute-start(f32[2,2,64,768]{3,2,1,0:T(8,128)} %add.48), channel_id=1, source_target_pairs={{0,2},{1,7},{2,0},{3,5},{4,6},{5,3},{6,4},{7,1},{8,10},{9,15},{10,... | collective-permute-start | bytes 2359304 | tf_op jit(solution)/shard_map/ppermute | solution.py:294
  82.5 7.8 %all-to-all-done = f32[16,64,128]{2,1,0:T(8,128)} async-done(((f32[16,64,128]{2,1,0:T(8,128)}), f32[16,64,128]{2,1,0:T(8,128)}, u32[]{:S(2)}, u32[]{:S(2)}) %all-to-all-start) | async-done | bytes 524320 | tf_op jit(solution)/shard_map/all_to_all | solution.py:365
  90.3 1.1 reduce_sum.18
  92.1 8.8 %all-to-all-start.1 = ((f32[8,64,128]{2,1,0:T(8,128)}), f32[8,64,128]{2,1,0:T(8,128)S(1)}, u32[]{:S(2)}, u32[]{:S(2)}) async-start(f32[8,64,128]{2,1,0:T(8,128)} %broadcast_in_dim.14), calls=%async_computation.1 | async-start | bytes 524288 | tf_op jit(solution)/shard_map/all_to_all | solution.py:367
  100.9 2.1 %add.43 = f32[2,2,64,768]{3,2,1,0:T(8,128)} add(f32[2,2,64,768]{3,2,1,0:T(8,128)S(1)} %get-tuple-element.20, f32[2,2,64,768]{3,2,1,0:T(8,128)} %collective-permute-done.9) | non-fusion elementwise | flops 196608 | bytes 2359296 | tf_op jit(solution)/shard_map/add | solution.py:305
  103.7 6.3 %all-to-all-done.1 = f32[8,64,128]{2,1,0:T(8,128)S(1)} async-done(((f32[8,64,128]{2,1,0:T(8,128)}), f32[8,64,128]{2,1,0:T(8,128)S(1)}, u32[]{:S(2)}, u32[]{:S(2)}) %all-to-all-start.1) | async-done | bytes 262176 | tf_op jit(solution)/shard_map/all_to_all | solution.py:367
  110.0 1.3 add_add_fusion
  111.3 1.4 collective-permute-start.16
  112.7 6.8 %collective-permute-done.10 = f32[2,2,64,768]{3,2,1,0:T(8,128)} collective-permute-done((f32[2,2,64,768]{3,2,1,0:T(8,128)}, f32[2,2,64,768]{3,2,1,0:T(8,128)}, u32[]{:S(2)}, u32[]{:S(2)}) %collective-permute-start.10) | collective-permute-done | bytes 786464 | tf_op jit(solution)/shard_map/ppermute | solution.py:294
  119.5 1.5 %add_add_fusion.1 = f32[2,2,64,768]{3,2,1,0:T(8,128)S(1)} fusion(f32[2,2,64,768]{3,2,1,0:T(8,128)} %collective-permute-done.10, f32[2,2,64,768]{3,2,1,0:T(8,128)S(1)} %get-tuple-element.18, f32[2,2,64,768]{3,2,1,0:T(8,128)} %collective-permute-done.8), kind=kLoop, calls=%fused_computation.2 | loop fusion | flops 393216 | bytes 3145728 | tf_op jit(solution)/shard_map/add | solution.py:306
  122.0 4.9 %all-to-all-start.2 = ((f32[16,64,128]{2,1,0:T(8,128)}), f32[16,64,128]{2,1,0:T(8,128)S(1)}, u32[]{:S(2)}, u32[]{:S(2)}) async-start(f32[16,64,128]{2,1,0:T(8,128)} %broadcast_in_dim.15), calls=%async_computation.2 | async-start | bytes 1048576 | tf_op jit(solution)/shard_map/all_to_all | solution.py:369
  128.0 3.8 %collective-permute-start.17 = (f32[2,64,256]{2,1,0:T(8,128)S(1)}, f32[2,64,256]{2,1,0:T(8,128)S(1)}, u32[]{:S(2)}, u32[]{:S(2)}) collective-permute-start(f32[2,64,256]{2,1,0:T(8,128)S(1)} %slice.56), channel_id=1, source_target_pairs={{0,8},{8,16},{16,24},{24,32},{32,40},{40,48},{48,56},{56,64},{64,7... | collective-permute-start | bytes 393224 | tf_op jit(solution)/shard_map/ppermute | solution.py:299
  131.8 1.5 %collective-permute-done.11 = f32[2,64,768]{2,1,0:T(8,128)S(1)} collective-permute-done((f32[2,64,768]{2,1,0:T(8,128)S(1)}, f32[2,64,768]{2,1,0:T(8,128)S(1)}, u32[]{:S(2)}, u32[]{:S(2)}) %collective-permute-start.11) | collective-permute-done | bytes 393248 | tf_op jit(solution)/shard_map/ppermute | solution.py:294
  133.4 1.9 %collective-permute-start.12 = (f32[2,64,256]{2,1,0:T(8,128)S(1)}, f32[2,64,256]{2,1,0:T(8,128)S(1)}, u32[]{:S(2)}, u32[]{:S(2)}) collective-permute-start(f32[2,64,256]{2,1,0:T(8,128)S(1)} %slice.51), channel_id=1, source_target_pairs={{0,8},{8,16},{16,24},{24,32},{32,40},{40,48},{48,56},{56,64},{64,7... | collective-permute-start | bytes 393224 | tf_op jit(solution)/shard_map/ppermute | solution.py:299
  135.3 3.1 %all-to-all-done.2 = f32[16,64,128]{2,1,0:T(8,128)S(1)} async-done(((f32[16,64,128]{2,1,0:T(8,128)}), f32[16,64,128]{2,1,0:T(8,128)S(1)}, u32[]{:S(2)}, u32[]{:S(2)}) %all-to-all-start.2) | async-done | bytes 524320 | tf_op jit(solution)/shard_map/all_to_all | solution.py:369
  138.7 3.6 %collective-permute-done.12 = f32[2,64,256]{2,1,0:T(8,128)S(1)} collective-permute-done((f32[2,64,256]{2,1,0:T(8,128)S(1)}, f32[2,64,256]{2,1,0:T(8,128)S(1)}, u32[]{:S(2)}, u32[]{:S(2)}) %collective-permute-start.12) | collective-permute-done | bytes 131104 | tf_op jit(solution)/shard_map/ppermute | solution.py:299
  (87 shorter events, 15.7 us)
Async XLA Ops:
  0.6 24.1 %copy-start.19 = (s32[1,1,2,2]{3,2,1,0:T(2,128)S(1)}, s32[1,1,2,2]{3,2,1,0:T(2,128)}, u32[]{:S(2)}) copy-start(s32[1,1,2,2]{3,2,1,0:T(2,128)} %param.16) | copy-start | bytes 52
  0.7 27.7 %copy-start.1 = (f32[2,2,256,256]{3,2,1,0:T(8,128)S(1)}, f32[2,2,256,256]{3,2,1,0:T(8,128)}, u32[]{:S(2)}) copy-start(f32[2,2,256,256]{3,2,1,0:T(8,128)} %probe.3) | copy-start | bytes 3145732
  0.7 27.7 %copy-start.8 = (f32[2,256,256]{2,1,0:T(8,128)S(1)}, f32[2,256,256]{2,1,0:T(8,128)}, u32[]{:S(2)}) copy-start(f32[2,256,256]{2,1,0:T(8,128)} %constant.48.clone.transfer) | copy-start | bytes 1572868
  6.4 10.9 %collective-permute-start.4 = (f32[2,128,256]{2,1,0:T(8,128)S(1)}, f32[2,128,256]{2,1,0:T(8,128)S(1)}, u32[]{:S(2)}, u32[]{:S(2)}) collective-permute-start(f32[2,128,256]{2,1,0:T(8,128)S(1)} %dynamic-slice_bitcast_fusion), channel_id=1, source_target_pairs={{8,0},{16,8},{24,16},{32,24},{40,32},{48,40},{56,48},{64,56},{72,6... | collective-permute-start | bytes 786440 | tf_op jit(solution)/shard_map/ppermute | solution.py:299
  11.6 10.4 %collective-permute-start = (f32[2,128,256]{2,1,0:T(8,128)S(1)}, f32[2,128,256]{2,1,0:T(8,128)S(1)}, u32[]{:S(2)}, u32[]{:S(2)}) collective-permute-start(f32[2,128,256]{2,1,0:T(8,128)S(1)} %dynamic-slice_bitcast_fusion.1), channel_id=1, source_target_pairs={{8,0},{16,8},{24,16},{32,24},{40,32},{48,40},{56,48},{64,56},{72,6... | collective-permute-start | bytes 786440 | tf_op jit(solution)/shard_map/ppermute | solution.py:299
  17.3 6.7 %collective-permute-start.5 = (f32[2,128,256]{2,1,0:T(8,128)S(1)}, f32[2,128,256]{2,1,0:T(8,128)S(1)}, u32[]{:S(2)}, u32[]{:S(2)}) collective-permute-start(f32[2,128,256]{2,1,0:T(8,128)S(1)} %collective-permute-done.4.h0), channel_id=1, source_target_pairs={{0,2},{1,7},{2,0},{3,5},{4,6},{5,3},{6,4},{7,1},{8,10},{9,15},{10,... | collective-permute-start | bytes 786440 | tf_op jit(solution)/shard_map/ppermute | solution.py:294
  22.0 6.4 %collective-permute-start.1 = (f32[2,128,256]{2,1,0:T(8,128)S(1)}, f32[2,128,256]{2,1,0:T(8,128)S(1)}, u32[]{:S(2)}, u32[]{:S(2)}) collective-permute-start(f32[2,128,256]{2,1,0:T(8,128)S(1)} %collective-permute-done.h0), channel_id=1, source_target_pairs={{0,2},{1,7},{2,0},{3,5},{4,6},{5,3},{6,4},{7,1},{8,10},{9,15},{10,... | collective-permute-start | bytes 786440 | tf_op jit(solution)/shard_map/ppermute | solution.py:294
  23.5 4.8 %collective-permute-start.6 = (f32[2,128,256]{2,1,0:T(8,128)S(1)}, f32[2,128,256]{2,1,0:T(8,128)S(1)}, u32[]{:S(2)}, u32[]{:S(2)}) collective-permute-start(f32[2,128,256]{2,1,0:T(8,128)S(1)} %collective-permute-done.4.h0), channel_id=1, source_target_pairs={{0,1},{1,0},{2,3},{3,2},{4,5},{5,4},{6,7},{7,6},{8,9},{9,8},{10,11... | collective-permute-start | bytes 786440 | tf_op jit(solution)/shard_map/ppermute | solution.py:282
  24.0 4.3 %collective-permute-start.7 = (f32[2,128,256]{2,1,0:T(8,128)S(1)}, f32[2,128,256]{2,1,0:T(8,128)S(1)}, u32[]{:S(2)}, u32[]{:S(2)}) collective-permute-start(f32[2,128,256]{2,1,0:T(8,128)S(1)} %collective-permute-done.5.h1), channel_id=1, source_target_pairs={{0,1},{1,0},{2,3},{3,2},{4,5},{5,4},{6,7},{7,6},{8,9},{9,8},{10,11... | collective-permute-start | bytes 786440 | tf_op jit(solution)/shard_map/ppermute | solution.py:282
  24.9 12.2 %collective-permute-start.2 = (f32[2,128,256]{2,1,0:T(8,128)S(1)}, f32[2,128,256]{2,1,0:T(8,128)S(1)}, u32[]{:S(2)}, u32[]{:S(2)}) collective-permute-start(f32[2,128,256]{2,1,0:T(8,128)S(1)} %collective-permute-done.h0), channel_id=1, source_target_pairs={{0,1},{1,0},{2,3},{3,2},{4,5},{5,4},{6,7},{7,6},{8,9},{9,8},{10,11... | collective-permute-start | bytes 786440 | tf_op jit(solution)/shard_map/ppermute | solution.py:282
  28.3 8.7 %copy-start.6 = (f32[2,128,256]{2,1,0:T(8,128)}, f32[2,128,256]{2,1,0:T(8,128)S(1)}, u32[]{:S(2)}) copy-start(f32[2,128,256]{2,1,0:T(8,128)S(1)} %collective-permute-done.1.h1) | copy-start | bytes 786436
  28.3 8.7 %collective-permute-start.3 = (f32[2,128,256]{2,1,0:T(8,128)S(1)}, f32[2,128,256]{2,1,0:T(8,128)S(1)}, u32[]{:S(2)}, u32[]{:S(2)}) collective-permute-start(f32[2,128,256]{2,1,0:T(8,128)S(1)} %collective-permute-done.1.h1), channel_id=1, source_target_pairs={{0,1},{1,0},{2,3},{3,2},{4,5},{5,4},{6,7},{7,6},{8,9},{9,8},{10,11... | collective-permute-start | bytes 786440 | tf_op jit(solution)/shard_map/ppermute | solution.py:282
  32.6 4.5 %copy-start.17 = (bf16[256,768]{1,0:T(8,128)(2,1)S(1)}, bf16[256,768]{1,0:T(8,128)(2,1)}, u32[]{:S(2)}) copy-start(bf16[256,768]{1,0:T(8,128)(2,1)} %constant.44.clone.fl) | copy-start | bytes 1179652
  38.1 9.0 %copy-start.2 = (f32[2,2,256,256]{3,2,1,0:T(8,128)S(1)}, f32[2,2,256,256]{3,2,1,0:T(8,128)}, u32[]{:S(2)}) copy-start(f32[2,2,256,256]{3,2,1,0:T(8,128)} %probe.3) | copy-start | bytes 3145732
  38.1 9.0 %copy-start.9 = (f32[2,256,256]{2,1,0:T(8,128)S(1)}, f32[2,256,256]{2,1,0:T(8,128)}, u32[]{:S(2)}) copy-start(f32[2,256,256]{2,1,0:T(8,128)} %constant.48.clone.transfer) | copy-start | bytes 1572868
  38.1 9.0 %copy-start.11 = (bf16[768,256]{1,0:T(8,128)(2,1)S(1)}, bf16[768,256]{1,0:T(8,128)(2,1)}, u32[]{:S(2)}) copy-start(bf16[768,256]{1,0:T(8,128)(2,1)} %constant.43.clone.tr) | copy-start | bytes 1179652
  38.1 9.0 %copy-start.13 = (bf16[256,768]{1,0:T(8,128)(2,1)S(1)}, bf16[256,768]{1,0:T(8,128)(2,1)}, u32[]{:S(2)}) copy-start(bf16[256,768]{1,0:T(8,128)(2,1)} %constant.42.clone.tl) | copy-start | bytes 1179652
  46.6 31.9 %collective-permute-start.14 = (f32[2,2,64,768]{3,2,1,0:T(8,128)}, f32[2,2,64,768]{3,2,1,0:T(8,128)}, u32[]{:S(2)}, u32[]{:S(2)}) collective-permute-start(f32[2,2,64,768]{3,2,1,0:T(8,128)} %get-tuple-element.25), channel_id=1, source_target_pairs={{0,1},{1,0},{2,3},{3,2},{4,5},{5,4},{6,7},{7,6},{8,9},{9,8},{10,11... | collective-permute-start | bytes 2359304 | tf_op jit(solution)/shard_map/ppermute | solution.py:282
  53.6 1.9 %collective-permute-start.18 = (f32[2,256,256]{2,1,0:T(8,128)S(1)}, f32[2,256,256]{2,1,0:T(8,128)S(1)}, u32[]{:S(2)}, u32[]{:S(2)}) collective-permute-start(f32[2,256,256]{2,1,0:T(8,128)S(1)} %get-tuple-element.27), channel_id=1, source_target_pairs={{0,1},{1,0},{2,3},{3,2},{4,5},{5,4},{6,7},{7,6},{8,9},{9,8},{10,11... | collective-permute-start | bytes 1572872 | tf_op jit(solution)/shard_map/ppermute | solution.py:282
  53.7 47.2 %collective-permute-start.9 = (f32[2,2,64,768]{3,2,1,0:T(8,128)}, f32[2,2,64,768]{3,2,1,0:T(8,128)}, u32[]{:S(2)}, u32[]{:S(2)}) collective-permute-start(f32[2,2,64,768]{3,2,1,0:T(8,128)} %get-tuple-element.21), channel_id=1, source_target_pairs={{0,1},{1,0},{2,3},{3,2},{4,5},{5,4},{6,7},{7,6},{8,9},{9,8},{10,11... | collective-permute-start | bytes 2359304 | tf_op jit(solution)/shard_map/ppermute | solution.py:282
  58.3 32.0 %all-to-all-start = ((f32[16,64,128]{2,1,0:T(8,128)}), f32[16,64,128]{2,1,0:T(8,128)}, u32[]{:S(2)}, u32[]{:S(2)}) async-start(f32[16,64,128]{2,1,0:T(8,128)} %reshape.20), calls=%async_computation | async-start | bytes 1048576 | tf_op jit(solution)/shard_map/all_to_all | solution.py:365
  78.4 31.5 %collective-permute-start.13 = (f32[2,2,64,768]{3,2,1,0:T(8,128)}, f32[2,2,64,768]{3,2,1,0:T(8,128)}, u32[]{:S(2)}, u32[]{:S(2)}) collective-permute-start(f32[2,2,64,768]{3,2,1,0:T(8,128)} %copy-done.3), channel_id=1, source_target_pairs={{0,1},{1,0},{2,3},{3,2},{4,5},{5,4},{6,7},{7,6},{8,9},{9,8},{10,11... | collective-permute-start | bytes 2359304 | tf_op jit(solution)/shard_map/ppermute | solution.py:282
  80.7 29.3 %collective-permute-start.15 = (f32[2,2,64,768]{3,2,1,0:T(8,128)}, f32[2,2,64,768]{3,2,1,0:T(8,128)S(1)}, u32[]{:S(2)}, u32[]{:S(2)}) collective-permute-start(f32[2,2,64,768]{3,2,1,0:T(8,128)} %add.48), channel_id=1, source_target_pairs={{0,2},{1,7},{2,0},{3,5},{4,6},{5,3},{6,4},{7,1},{8,10},{9,15},{10,... | collective-permute-start | bytes 2359304 | tf_op jit(solution)/shard_map/ppermute | solution.py:294
  92.1 17.8 %all-to-all-start.1 = ((f32[8,64,128]{2,1,0:T(8,128)}), f32[8,64,128]{2,1,0:T(8,128)S(1)}, u32[]{:S(2)}, u32[]{:S(2)}) async-start(f32[8,64,128]{2,1,0:T(8,128)} %broadcast_in_dim.14), calls=%async_computation.1 | async-start | bytes 524288 | tf_op jit(solution)/shard_map/all_to_all | solution.py:367
  100.9 11.8 %collective-permute-start.8 = (f32[2,2,64,768]{3,2,1,0:T(8,128)}, f32[2,2,64,768]{3,2,1,0:T(8,128)}, u32[]{:S(2)}, u32[]{:S(2)}) collective-permute-start(f32[2,2,64,768]{3,2,1,0:T(8,128)} %copy-done.4), channel_id=1, source_target_pairs={{0,1},{1,0},{2,3},{3,2},{4,5},{5,4},{6,7},{7,6},{8,9},{9,8},{10,11... | collective-permute-start | bytes 2359304 | tf_op jit(solution)/shard_map/ppermute | solution.py:282
  103.0 16.5 %collective-permute-start.10 = (f32[2,2,64,768]{3,2,1,0:T(8,128)}, f32[2,2,64,768]{3,2,1,0:T(8,128)}, u32[]{:S(2)}, u32[]{:S(2)}) collective-permute-start(f32[2,2,64,768]{3,2,1,0:T(8,128)} %add.43), channel_id=1, source_target_pairs={{0,2},{1,7},{2,0},{3,5},{4,6},{5,3},{6,4},{7,1},{8,10},{9,15},{10,... | collective-permute-start | bytes 2359304 | tf_op jit(solution)/shard_map/ppermute | solution.py:294
  111.3 15.7 %collective-permute-start.16 = (f32[2,64,768]{2,1,0:T(8,128)S(1)}, f32[2,64,768]{2,1,0:T(8,128)}, u32[]{:S(2)}, u32[]{:S(2)}) collective-permute-start(f32[2,64,768]{2,1,0:T(8,128)S(1)} %slice_bitcast_fusion), channel_id=1, source_target_pairs={{0,6},{1,3},{2,4},{3,1},{4,2},{5,7},{6,0},{7,5},{8,14},{9,11},{10,... | collective-permute-start | bytes 1179656 | tf_op jit(solution)/shard_map/ppermute | solution.py:294
  121.1 12.2 %collective-permute-start.11 = (f32[2,64,768]{2,1,0:T(8,128)S(1)}, f32[2,64,768]{2,1,0:T(8,128)S(1)}, u32[]{:S(2)}, u32[]{:S(2)}) collective-permute-start(f32[2,64,768]{2,1,0:T(8,128)S(1)} %slice_bitcast_fusion.2), channel_id=1, source_target_pairs={{0,6},{1,3},{2,4},{3,1},{4,2},{5,7},{6,0},{7,5},{8,14},{9,11},{10,... | collective-permute-start | bytes 1179656 | tf_op jit(solution)/shard_map/ppermute | solution.py:294
  122.0 16.4 %all-to-all-start.2 = ((f32[16,64,128]{2,1,0:T(8,128)}), f32[16,64,128]{2,1,0:T(8,128)S(1)}, u32[]{:S(2)}, u32[]{:S(2)}) async-start(f32[16,64,128]{2,1,0:T(8,128)} %broadcast_in_dim.15), calls=%async_computation.2 | async-start | bytes 1048576 | tf_op jit(solution)/shard_map/all_to_all | solution.py:369
  128.0 10.7 %collective-permute-start.17 = (f32[2,64,256]{2,1,0:T(8,128)S(1)}, f32[2,64,256]{2,1,0:T(8,128)S(1)}, u32[]{:S(2)}, u32[]{:S(2)}) collective-permute-start(f32[2,64,256]{2,1,0:T(8,128)S(1)} %slice.56), channel_id=1, source_target_pairs={{0,8},{8,16},{16,24},{24,32},{32,40},{40,48},{48,56},{56,64},{64,7... | collective-permute-start | bytes 393224 | tf_op jit(solution)/shard_map/ppermute | solution.py:299
  133.4 9.0 %collective-permute-start.12 = (f32[2,64,256]{2,1,0:T(8,128)S(1)}, f32[2,64,256]{2,1,0:T(8,128)S(1)}, u32[]{:S(2)}, u32[]{:S(2)}) collective-permute-start(f32[2,64,256]{2,1,0:T(8,128)S(1)} %slice.51), channel_id=1, source_target_pairs={{0,8},{8,16},{16,24},{24,32},{32,40},{40,48},{48,56},{56,64},{64,7... | collective-permute-start | bytes 393224 | tf_op jit(solution)/shard_map/ppermute | solution.py:299
  138.6 4.7 %collective-permute-start.19 = (f32[2,256,256]{2,1,0:T(8,128)S(1)}, f32[2,256,256]{2,1,0:T(8,128)S(1)}, u32[]{:S(2)}, u32[]{:S(2)}) collective-permute-start(f32[2,256,256]{2,1,0:T(8,128)S(1)} %reshape.21), channel_id=1, source_target_pairs={{0,1},{1,0},{2,3},{3,2},{4,5},{5,4},{6,7},{7,6},{8,9},{9,8},{10,11... | collective-permute-start | bytes 1572872 | tf_op jit(solution)/shard_map/ppermute | solution.py:282
  (11 other events, 29.2 us)

commit v2 on v0

v2 whole, which is shorter than its diff:
```python
import math

import jax
import jax.numpy as jnp
import ml_dtypes
import numpy as np
from jax import lax
from jax.experimental import pallas as pl
from jax.experimental.pallas import tpu as pltpu
from jax.sharding import PartitionSpec as P

BF = jnp.bfloat16
F32 = jnp.float32
LONG = 1 << 35


def split_table(table):
    high = table.astype(ml_dtypes.bfloat16)
    low = (table - high.astype(np.float64)).astype(ml_dtypes.bfloat16)
    return high, low


def make_tables(n):
    h = n // 2
    even = np.concatenate([np.arange(0, h, 2), [h], np.arange(n - 2, h, -2)])
    odd = np.concatenate([np.arange(1, h, 2), np.arange(n - 1, h, -2)])
    order = np.concatenate([even, odd])
    pixel = np.arange(n)
    blocks = []
    for rows in (even, odd):
        phase = 2 * np.pi * ((rows[:, None] * pixel[None, :h]) % n) / n
        blocks.append((np.cos(phase) + np.sin(phase)) / math.sqrt(n))

    def square(block):
        high, low = split_table(block)
        half = np.concatenate([high, low], 1)
        return np.concatenate([half, half], 0)

    squares = []
    for block in blocks:
        squares += [square(block.T).T, square(block.T), square(block).T, square(block)]
    perm = np.zeros((n, n))
    perm[pixel, order] = 1
    squares.append(perm.astype(ml_dtypes.bfloat16))
    f = (order + h) % n - h
    q = (f[:, None] ** 2 + f[None, :] ** 2) % (4 * n)
    chirp = 2 * np.pi * q / (4 * n)
    transfer = np.stack([np.cos(chirp), -np.sin(chirp)]).astype(np.float32)
    return np.stack(squares), transfer


def split(x):
    high = x.astype(BF)
    return high, (x - high.astype(F32)).astype(BF)


def dot(a, b):
    return jnp.dot(a, b, preferred_element_type=F32)


def columns_by(x, table):
    high, low = split(x)
    y = dot(jnp.concatenate([high, low], 1), table)
    h = x.shape[1]
    return y[:, :h] + y[:, h:]


def rows_by(table, x):
    high, low = split(x)
    y = dot(table, jnp.concatenate([high, low], 0))
    h = x.shape[0]
    return y[:h] + y[h:]


def to_frequency(planes, tables):
    h = planes[0].shape[0] // 2
    even = [columns_by(x[:, :h] + x[:, h:], tables[1]) for x in planes]
    odd = [columns_by(x[:, :h] - x[:, h:], tables[5]) for x in planes]
    planes = [jnp.concatenate(p, 1) for p in zip(even, odd)]
    even = [rows_by(tables[0], x[:h] + x[h:]) for x in planes]
    odd = [rows_by(tables[4], x[:h] - x[h:]) for x in planes]
    return [jnp.concatenate(p, 0) for p in zip(even, odd)]


def to_pixels(planes, tables):
    h = planes[0].shape[0] // 2
    a = [columns_by(x[:, :h], tables[3]) for x in planes]
    b = [columns_by(x[:, h:], tables[7]) for x in planes]
    planes = [jnp.concatenate([p + q, p - q], 1) for p, q in zip(a, b)]
    a = [rows_by(tables[2], x[:h]) for x in planes]
    b = [rows_by(tables[6], x[h:]) for x in planes]
    return [jnp.concatenate([p + q, p - q], 0) for p, q in zip(a, b)]


def cmul(a, b):
    return a[0] * b[0] - a[1] * b[1], a[0] * b[1] + a[1] * b[0]


def cmulc(a, b):
    return a[0] * b[0] + a[1] * b[1], a[1] * b[0] - a[0] * b[1]


def swap_rows(z):
    q = z.shape[0] // 4
    row = lax.broadcasted_iota(jnp.int32, z.shape, 0)
    fixed = jnp.logical_or(row == 0, row == q)
    turned = jnp.concatenate([z[q : 2 * q], z[:q], z[3 * q :], z[2 * q : 3 * q]], 0)
    return jnp.where(fixed, z, turned)


def swap_cols(z):
    q = z.shape[1] // 4
    even, odd = z[:, : 2 * q], z[:, 2 * q :]
    col = lax.broadcasted_iota(jnp.int32, even.shape, 1)
    fixed = jnp.logical_or(col == 0, col == q)
    even = jnp.where(fixed, even, pltpu.roll(even, q, 1))
    return jnp.concatenate([even, pltpu.roll(odd, q, 1)], 1)


def mix(pair, sign):
    a, b = pair
    ca, cb = swap_cols(a), swap_cols(b)
    re = 0.5 * (sign * (b - swap_rows(cb)) + (swap_rows(a) + ca))
    im = 0.5 * (sign * (swap_rows(ca) - a) + (swap_rows(b) + cb))
    return re, im


def corner_of(r, c, rows):
    row = jnp.minimum(lax.div(r, 8), rows // 8 - 33) * 8
    col = lax.div(c, 128) * 128
    return pl.multiple_of(row, 8), pl.multiple_of(col, 128), r - row, c - col


def partners(y, c):
    near, far = jnp.bitwise_xor(y, 1), 3 - y
    return jnp.where(c == 0, near, far), jnp.where(c == 0, far, near), 3 - near


def plan_kernel(info, me, plan, token):
    count = [info[s, 0, 0] for s in range(8)]
    zeros, doubles = jnp.int32(0), jnp.int32(0)
    zero_rank, double_rank = [], []
    for s in range(8):
        zero_rank.append(zeros)
        double_rank.append(doubles)
        zeros = zeros + (count[s] == 0).astype(jnp.int32)
        doubles = doubles + (count[s] == 2).astype(jnp.int32)
    for s in range(8):
        source = jnp.int32(0)
        for e in range(8):
            taken = jnp.logical_and(count[e] == 2, double_rank[e] == zero_rank[s])
            source = jnp.where(taken, e, source)
        away = count[s] == 0
        source = jnp.where(away, source, s)
        slot = away.astype(jnp.int32)
        plan[s, 0] = source
        plan[s, 1] = slot
        plan[s, 2] = info[source, 0, 1 + 2 * slot]
        plan[s, 3] = info[source, 0, 2 + 2 * slot]
    token[...] = jnp.zeros_like(token)
    plan[8, 0] = me[0, 5]
    plan[8, 1] = me[0, 6]


def pick_kernel(plan, mine_1, got_a, got_b, for_sib, sem):
    y, c = plan[8, 0], plan[8, 1]
    source = plan[2 * y + 1 - c, 0]
    a, b, e = partners(y, c)

    def give(device, ref):
        @pl.when(source == device)
        def _():
            copy = pltpu.make_async_copy(ref, for_sib, sem)
            copy.start()
            copy.wait()

    give(2 * y + c, mine_1)
    give(2 * a + c, got_a)
    give(2 * b + c, got_b.at[0])
    give(2 * e + c, got_b.at[1])


def tie_kernel(*refs):
    pass


def join_kernel(*refs):
    refs[-1][...] = jnp.zeros_like(refs[-1])


def compute_kernel(
    plan, joined, strip, h00, h01, h02, h03, h10, h11, h12, h13, probe,
    mine_0, mine_1, got_a, got_b, got_sib, tables, transfer,
    grad, mine, sib, halo, full, obj, us, psi, meas, sem,
):
    y, c = plan[8, 0], plan[8, 1]
    own = 2 * y + c
    source, slot = plan[own, 0], plan[own, 1]
    row, col, dr, dc = corner_of(plan[own, 2], plan[own, 3], 512)
    first = lax.div(col, 128)

    a, b, e = partners(y, c)
    core = lax.rem(source, 2)
    chip = lax.div(source, 2)
    here = jnp.logical_and(slot == 1, core == c)
    choices = [
        (slot == 0, mine_0),
        (jnp.logical_and(here, chip == y), mine_1),
        (jnp.logical_and(here, chip == a), got_a),
        (jnp.logical_and(here, chip == b), got_b.at[0]),
        (jnp.logical_and(here, chip == e), got_b.at[1]),
        (jnp.logical_and(slot == 1, core != c), got_sib),
    ]
    for chosen, ref in choices:

        @pl.when(chosen)
        def _():
            pltpu.make_async_copy(ref, meas, sem).start()

    half = lax.rem(y, 2)
    for layer, pieces in enumerate(((h00, h01, h02, h03), (h10, h11, h12, h13))):
        for k, piece in enumerate(pieces):
            hh = half if k % 2 == 0 else 1 - half
            cc = c if k < 2 else 1 - c
            at = pl.multiple_of(256 * hh + 128 * cc, 128)
            halo[:, layer, pl.ds(at, 128), :] = piece[...]
    for i in range(3):

        @pl.when(first + i >= 4)
        def _():
            cols = pl.multiple_of(128 * (first + i - 4), 128)
            full[:, :, :, 128 * i : 128 * (i + 1)] = halo[:, :, pl.ds(row, 264), pl.ds(cols, 128)]

        @pl.when(first + i < 4)
        def _():
            cols = pl.multiple_of(col + 128 * i, 128)
            full[:, :, :, 128 * i : 128 * (i + 1)] = strip[:, :, pl.ds(row, 264), pl.ds(cols, 128)]

    def window(layer):
        for part in range(2):
            x = pltpu.roll(full[part, layer], lax.rem(384 - dc, 384), 1)[:, :256]
            x = pltpu.roll(x, lax.rem(264 - dr, 264), 0)
            obj[layer, part] = x[:256]

    def load(ref, *index):
        return ref[(*index, 0)], ref[(*index, 1)]

    def modes(planes):
        return (planes[0], planes[1]), (planes[2], planes[3])

    def chirped(product, planes):
        h = (transfer[0], transfer[1])
        return [x for pair in modes(planes) for x in product(pair, h)]

    window(0)
    planes = [x for m in range(2) for x in cmul((probe[0, m], probe[1, m]), load(obj, 0))]
    planes = to_pixels(chirped(cmul, to_frequency(planes, tables)), tables)
    for k in range(4):
        us[k // 2, k % 2] = planes[k]
    window(1)
    pltpu.make_async_copy(mine_0, meas, sem).wait()
    pm = tables[8]
    high, low = split(meas[...])
    high, low = split(dot(pm, high) + dot(pm, low))
    dims = (((1,), (1,)), ((), ()))
    misfit = -(
        lax.dot_general(high, pm, dims, preferred_element_type=F32)
        + lax.dot_general(low, pm, dims, preferred_element_type=F32)
    )
    planes = [x for m in range(2) for x in cmul(load(us, m), load(obj, 1))]
    planes = to_frequency(planes, tables)
    for m, pair in enumerate(modes(planes)):
        re, im = mix(pair, 1.0)
        psi[m, 0] = re
        psi[m, 1] = im
        misfit = misfit + (re * re + im * im)
    meas[...] = misfit
    planes = [
        x for m in range(2) for x in mix((psi[m, 0] * meas[...], psi[m, 1] * meas[...]), -1.0)
    ]
    planes = to_pixels(planes, tables)
    back = []
    total = None
    for m, pair in enumerate(modes(planes)):
        term = cmulc(pair, load(us, m))
        total = term if total is None else (total[0] + term[0], total[1] + term[1])
        back += cmulc(pair, load(obj, 1))
    grad[0, 1] = total[0]
    grad[1, 1] = total[1]
    planes = to_pixels(chirped(cmulc, to_frequency(back, tables)), tables)
    total = None
    for m, pair in enumerate(modes(planes)):
        last = cmulc(pair, load(obj, 0))

        @pl.when(c == m)
        def _():
            mine[0] = last[0]
            mine[1] = last[1]

        @pl.when(c != m)
        def _():
            sib[0] = last[0]
            sib[1] = last[1]

        term = cmulc(pair, (probe[0, m], probe[1, m]))
        total = term if total is None else (total[0] + term[0], total[1] + term[1])
    grad[0, 0] = total[0]
    grad[1, 0] = total[1]


def rows_kernel(plan, g0, g1, before, msg, kept, token, tall):
    y, c = plan[8, 0], plan[8, 1]
    a, b, e = partners(y, c)
    tall[:, :72] = jnp.zeros((4, 72, 256), F32)
    tall[:, 328:] = jnp.zeros((4, 72, 256), F32)
    for w, g in enumerate((g0, g1)):
        core = c if w == 0 else 1 - c
        r = plan[2 * y + core, 2]
        for plane in range(4):
            tall[plane, 72:328] = g[plane // 2, plane % 2]

        def put(out, chip):
            start = jnp.clip(72 + 128 * chip + 64 * c - r, 0, 328)
            row = lax.div(start, 8) * 8
            shift = start - row
            row = pl.multiple_of(row, 8)
            for plane in range(4):
                x = pltpu.roll(tall[plane, pl.ds(row, 72), :], lax.rem(72 - shift, 72), 0)
                out[plane] = x[:64]

        put(msg.at[w, 0], a)
        put(msg.at[w, 1], e)
        put(kept.at[w, 0], y)
        put(kept.at[w, 1], b)
    token[...] = before[...]


def place_kernel(
    plan, kept, got, before, send_edge, send_strip, keep_edge, keep_strip, token, acc
):
    y, c = plan[8, 0], plan[8, 1]
    a, _, _ = partners(y, c)
    acc[...] = jnp.zeros_like(acc)
    for k in range(4):
        ref, w = (kept, k) if k < 2 else (got, k - 2)
        chip = y if k < 2 else a
        core = c if w == 0 else 1 - c
        _, col, _, dc = corner_of(jnp.int32(0), plan[2 * chip + core, 3], 512)
        for d in range(2):
            for plane in range(4):
                x = jnp.concatenate([ref[w, d, plane], jnp.zeros((64, 128), F32)], 1)
                acc[d, plane, :, pl.ds(col, 384)] += pltpu.roll(x, dc, 1)
    keep_strip[...] = acc[0, :, :, :512]
    keep_edge[...] = acc[0, :, :, 512:]
    send_strip[...] = acc[1, :, :, :512]
    send_edge[...] = acc[1, :, :, 512:]
    token[...] = before[...]


def spread_kernel(scale, x, before, out, token):
    total = x[0]
    for k in range(1, x.shape[0]):
        total = total + x[k]
    total = total * scale
    for k in range(out.shape[0]):
        out[k] = total
    token[...] = before[...]


def stack_kernel(core, x, y, out):
    for part in range(2):
        out[part, core[0]] = x[part]
        out[part, 1 - core[0]] = y[part]


def add_kernel(x, y, before, out, token):
    out[...] = x[...] + y[...]
    token[...] = before[...]


def struct(*shape):
    return jax.ShapeDtypeStruct(shape, F32)


SMEM = pl.BlockSpec(memory_space=pltpu.SMEM)
VMEM = pl.BlockSpec(memory_space=pltpu.VMEM)
HBM = pl.BlockSpec(memory_space=pltpu.HBM)
ANY = pl.BlockSpec(memory_space=pl.ANY)


def run_kernel(body, name, ins, in_specs, outs, out_specs, scratch, flops, size, moved=1):
    return pl.pallas_call(
        body,
        out_shape=outs,
        in_specs=in_specs,
        out_specs=out_specs,
        scratch_shapes=scratch,
        compiler_params=pltpu.CompilerParams(vmem_limit_bytes=size << 20),
        cost_estimate=pl.CostEstimate(flops=flops, bytes_accessed=moved << 18, transcendentals=0),
        name=name,
    )(*ins)


def tied(x, *others):
    return pl.pallas_call(
        tie_kernel,
        out_shape=jax.ShapeDtypeStruct(x.shape, x.dtype),
        in_specs=[VMEM] * (1 + len(others)),
        out_specs=VMEM,
        input_output_aliases={0: 0},
        compiler_params=pltpu.CompilerParams(vmem_limit_bytes=4 << 20),
        name="tied",
    )(x, *others)


def pairs(n, f):
    return [(i, f(i)) for i in range(n)]


def core_swap(x):
    return lax.ppermute(x, "c", [(0, 1), (1, 0)])


def y_swap(x, first):
    def partner(i):
        y, c = i // 2, i % 2
        return 2 * ((y ^ 1) if (c == 0) == first else 3 - y) + c

    return lax.ppermute(x, ("y", "c"), pairs(8, partner))


def tile_shift(x, by):
    n = lax.axis_size("z") * lax.axis_size("x")
    return lax.ppermute(x, ("z", "x"), [(i, i + by) for i in range(n) if 0 <= i + by < n])


TOKEN = jax.ShapeDtypeStruct((8, 128), F32)


def spread(x, copies, scale, token):
    _, rows, cols = x.shape

    def body(*refs):
        spread_kernel(scale, *refs)

    return run_kernel(
        body, "spread", (x, token), [VMEM] * 2,
        [struct(copies, rows, cols), TOKEN], [VMEM] * 2, [], 1 << 20, 4,
    )


def added(x, y, token):
    return run_kernel(
        add_kernel, "added", (x, y, token), [VMEM] * 3,
        [struct(*x.shape), TOKEN], [VMEM] * 2, [], 1 << 20, 4,
    )


def shards(object_field, probe, measured, offsets, counts):
    n = probe.shape[-1]
    tables, transfer = make_tables(n)
    y, c = lax.axis_index("y").astype(jnp.int32), lax.axis_index("c").astype(jnp.int32)
    zero = jnp.zeros((), jnp.int32)

    row = 256 * lax.rem(y, 2) + 128 * c
    parts = []
    for layer in range(2):
        part = lax.dynamic_slice(
            object_field, (zero, jnp.int32(layer), row, zero), (2, 1, 128, n)
        ).reshape(2, 128, n)
        parts.append(part)
    parts, measured, offsets, counts = lax.optimization_barrier(
        (parts, measured, offsets, counts)
    )
    halos = [tile_shift(part, -1) for part in parts]

    own_row = jnp.concatenate([counts.reshape(1), offsets.reshape(4), y[None], c[None]])
    own_row = jnp.pad(own_row, (0, 121))
    info = lax.all_to_all(jnp.broadcast_to(own_row, (8, 8, 128)), ("y", "c"), 0, 0, tiled=True)
    own_row = jnp.broadcast_to(own_row, (8, 128))

    mine_0, mine_1 = measured[0, 0, 0], measured[0, 0, 1]
    got_a = y_swap(mine_1, True)
    got_b = y_swap(jnp.stack([mine_1, got_a]), False)
    plan, planned = run_kernel(
        plan_kernel, "plan", (info, own_row), [SMEM] * 2,
        [jax.ShapeDtypeStruct((9, 4), jnp.int32), struct(8, 128)], [SMEM, VMEM],
        [], 1 << 20, 4,
    )
    for_sib = run_kernel(
        pick_kernel, "pick", (plan, mine_1, got_a, got_b), [SMEM, ANY, ANY, ANY],
        struct(n, n), ANY, [pltpu.SemaphoreType.DMA(())], 1 << 20, 4,
    )
    got_sib = core_swap(for_sib)

    pieces = []
    halos[0] = tied(halos[0], planned)
    for got in halos:
        other = y_swap(got, True)
        pieces += [got, other, core_swap(got), core_swap(other)]

    joined = run_kernel(
        join_kernel, "joined", tuple(pieces), [ANY] * 8, struct(8, 128), VMEM, [], LONG, 4,
    )
    grad, mine, sib = run_kernel(
        compute_kernel, "position",
        (plan, joined, object_field, *pieces, probe, mine_0, mine_1, got_a, got_b, got_sib,
         jnp.asarray(tables), jnp.asarray(transfer)),
        [SMEM] + [VMEM] * 11 + [ANY] * 5 + [VMEM] * 2,
        [struct(2, 2, n, n), struct(2, n, n), struct(2, n, n)], [VMEM] * 3,
        [pltpu.VMEM((2, 2, 512, n), F32), pltpu.VMEM((2, 2, 264, 384), F32)]
        + [pltpu.VMEM((2, 2, n, n), F32)] * 3
        + [pltpu.VMEM((n, n), F32), pltpu.SemaphoreType.DMA(())],
        48 * 3 * 2 * n**3, 24, 64,
    )

    grad_sib = core_swap(grad)
    total, token = added(mine, core_swap(sib), jnp.zeros((8, 128), F32))
    pieces_1 = lax.all_to_all(total.reshape(16, 32, n), ("x", "y"), 0, 0, tiled=True)
    msg, kept, token = run_kernel(
        rows_kernel, "rows", (plan, grad, grad_sib, token), [SMEM, VMEM, VMEM, VMEM],
        [struct(2, 2, 4, 64, n)] * 2 + [TOKEN], [VMEM] * 3, [pltpu.VMEM((4, 400, n), F32)],
        1 << 20, 12,
    )
    got = y_swap(msg, True)
    spread_1, token = spread(pieces_1, 8, 1.0, token)
    pieces_2 = lax.all_to_all(spread_1, "z", 0, 0, tiled=True)
    send_edge, send_strip, keep_edge, keep_strip, token = run_kernel(
        place_kernel, "place", (plan, kept, got, token), [SMEM, VMEM, VMEM, VMEM],
        [struct(4, 64, n), struct(4, 64, 512)] * 2 + [TOKEN], [VMEM] * 5,
        [pltpu.VMEM((2, 4, 64, 768), F32)], 1 << 20, 12,
    )
    got_edge = y_swap(send_edge, False)
    got_strip = y_swap(send_strip, False)
    edge, token = added(keep_edge, got_edge, token)
    edge = tile_shift(edge, 1)
    spread_2, token = spread(pieces_2, 16, 1.0 / 16.0, token)
    total = lax.all_to_all(spread_2, ("x", "y"), 0, 0, tiled=True).reshape(2, n, n)
    strip = keep_strip + got_strip
    rows = jnp.concatenate([strip[:, :, :n] + edge, strip[:, :, n:]], 2)
    other = core_swap(total)
    probe_gradient = run_kernel(
        stack_kernel, "stacked", (c[None], total, other), [SMEM, VMEM, VMEM],
        struct(2, 2, n, n), VMEM, [], LONG, 4,
    )
    return rows.reshape(2, 2, 64, 512), probe_gradient


def solution(mesh):
    sizes = (8, 4, 4, 2)
    split_mesh = jax.sharding.Mesh(mesh.devices.reshape(sizes), ("z", "x", "y", "c"))
    tile, scan = ("z", "x"), ("y", "c")
    in_specs = (
        P(None, None, None, tile),
        P(),
        P(tile, scan, None, None, None),
        P(tile, scan, None, None),
        P(tile, scan),
    )
    out_specs = (P(None, None, scan, tile), P())
    return jax.shard_map(
        shards, mesh=split_mesh, in_specs=in_specs, out_specs=out_specs, check_vma=False
    )
```

time: 544 us -> 117 us (0.22)
  the two profiles are of different devices: /device:TPU:2 before, /device:TPU:32 now
where the time goes in v2:
time: 117 us
  starting transfers between devices  41.8 us (36%)
  waiting for transfers between devices  29.5 us (25%)
  blocking collectives  21.4 us (18%)
  Pallas kernels  16.6 us (14%)
  local copies, waits for them, and re-layouts  4.73 us (4%)
  between operations  1.48 us (1%)
    all_to_all x1, blocking collectives, shards(): lax.all_to_all(total.reshape(16, 32, n), ('x', 'y'), 0, 0, tiled=True)  21.4 us
    pallas_call x11, Pallas kernels, run_kernel(): pl.pallas_call(body, out_shape=outs, in_specs=in_specs, out_specs=out_spe...  16.6 us
    ppermute x7, waiting for transfers between devices, y_swap(): return lax.ppermute(x, ('y', 'c'), pairs(8, partner))  12.8 us
    ppermute x7, starting transfers between devices, y_swap(): return lax.ppermute(x, ('y', 'c'), pairs(8, partner))  12.3 us
    ppermute x3, starting transfers between devices, tile_shift(): lax.ppermute(x, ('z', 'x'), [(i, i + by) for i in range(n) if 0 <= i + by...  10.3 us
    all_to_all x1, waiting for transfers between devices, shards(): lax.all_to_all(spread_2, ('x', 'y'), 0, 0, tiled=True).reshape(2, n, n)  9.21 us
    all_to_all x1, starting transfers between devices, shards(): pieces_2 = lax.all_to_all(spread_1, 'z', 0, 0, tiled=True)  8.99 us
    ppermute x8, waiting for transfers between devices, core_swap(): return lax.ppermute(x, 'c', [(0, 1), (1, 0)])  4.99 us
  transfers between devices with their start and end apart: 21, of which 10 were waited for; matrix products, arithmetic and copies ran while one was open for 2% of the time, Pallas kernels for 4%

profile of v2, /device:TPU:32, one launch (start us, length us, event | category | flops | bytes accessed | tf_op | source)
XLA Modules:
  0.0 116.6 jit_solution(13224297985445102953)
XLA Ops:
  0.6 1.1 dynamic-slice_bitcast_fusion
  1.7 1.1 slice_bitcast_fusion.1
  2.8 1.7 %collective-permute-start.8 = (f32[256,256]{1,0:T(8,128)S(1)}, f32[256,256]{1,0:T(8,128)S(1)}, u32[]{:S(2)}, u32[]{:S(2)}) collective-permute-start(f32[256,256]{1,0:T(8,128)S(1)} %get-tuple-element.57.mine_1), channel_id=1, source_target_pairs={{0,2},{1,7},{2,0},{3,5},{4,6},{5,3},{6,4},{7,1},{8,10},{9,15},{10,... | collective-permute-start | bytes 786440 | tf_op jit(solution)/shard_map/ppermute | solution.py:429
  4.5 4.2 %collective-permute-start = (f32[2,128,256]{2,1,0:T(8,128)S(1)}, f32[2,128,256]{2,1,0:T(8,128)S(1)}, u32[]{:S(2)}, u32[]{:S(2)}) collective-permute-start(f32[2,128,256]{2,1,0:T(8,128)S(1)} %get-tuple-element.30), channel_id=1, source_target_pairs={{8,0},{16,8},{24,16},{32,24},{40,32},{48,40},{56,48},{64,56},{72,6... | collective-permute-start | bytes 786440 | tf_op jit(solution)/shard_map/ppermute | solution.py:434
  8.7 2.7 %collective-permute-start.4 = (f32[2,128,256]{2,1,0:T(8,128)S(1)}, f32[2,128,256]{2,1,0:T(8,128)S(1)}, u32[]{:S(2)}, u32[]{:S(2)}) collective-permute-start(f32[2,128,256]{2,1,0:T(8,128)S(1)} %get-tuple-element.32), channel_id=1, source_target_pairs={{8,0},{16,8},{24,16},{32,24},{40,32},{48,40},{56,48},{64,56},{72,6... | collective-permute-start | bytes 786440 | tf_op jit(solution)/shard_map/ppermute | solution.py:434
  12.1 0.8 reshape.28
  13.6 4.2 %all-to-all-start = ((s32[8,8,128]{2,1,0:T(8,128)}), s32[8,8,128]{2,1,0:T(8,128)S(1)}, u32[]{:S(2)}, u32[]{:S(2)}) async-start(s32[8,8,128]{2,1,0:T(8,128)} %broadcast_in_dim.18), calls=%async_computation | async-start | bytes 65536 | tf_op jit(solution)/shard_map/all_to_all | solution.py:479
  17.8 3.3 %collective-permute-start.9 = (f32[2,256,256]{2,1,0:T(8,128)S(1)}, f32[2,256,256]{2,1,0:T(8,128)S(1)}, u32[]{:S(2)}, u32[]{:S(2)}) collective-permute-start(f32[2,256,256]{2,1,0:T(8,128)S(1)} %pad_maximum_fusion), channel_id=1, source_target_pairs={{0,6},{1,3},{2,4},{3,1},{4,2},{5,7},{6,0},{7,5},{8,14},{9,11},{10,... | collective-permute-start | bytes 1572872 | tf_op jit(solution)/shard_map/ppermute | solution.py:429
  21.1 2.2 %all-to-all-done.info = s32[8,8,128]{2,1,0:T(8,128)S(1)} async-done(((s32[8,8,128]{2,1,0:T(8,128)}), s32[8,8,128]{2,1,0:T(8,128)S(1)}, u32[]{:S(2)}, u32[]{:S(2)}) %all-to-all-start) | async-done | bytes 32800 | tf_op jit(solution)/shard_map/all_to_all | solution.py:479
  23.3 2.0 %plan.1 = (s32[9,4]{1,0:T(8,128)S(1)}, f32[8,128]{1,0:T(8,128)S(1)}) custom-call(s32[8,8,128]{2,1,0:T(8,128)S(1)} %all-to-all-done.info, s32[8,128]{1,0:T(8,128)S(1)} %broadcast_in_dim.19.me), custom_call_target="tpu_custom_call" | custom-call | flops 1048576 | bytes 262144 | tf_op jit(solution)/shard_map/plan/pallas_call | solution.py:392
  25.3 0.7 collective-permute-start.1
  26.0 1.4 %collective-permute-start.5 = (f32[2,128,256]{2,1,0:T(8,128)S(1)}, f32[2,128,256]{2,1,0:T(8,128)S(1)}, u32[]{:S(2)}, u32[]{:S(2)}) collective-permute-start(f32[2,128,256]{2,1,0:T(8,128)S(1)} %collective-permute-done.4.refs_4_.h10), channel_id=1, source_target_pairs={{0,2},{1,7},{2,0},{3,5},{4,6},{5,3},{6,4},{7,1},{8,10},{9,15},{10,... | collective-permute-start | bytes 786440 | tf_op jit(solution)/shard_map/ppermute | solution.py:429
  27.9 3.8 %collective-permute-done.1.refs_1_.h01 = f32[2,128,256]{2,1,0:T(8,128)S(1)} collective-permute-done((f32[2,128,256]{2,1,0:T(8,128)S(1)}, f32[2,128,256]{2,1,0:T(8,128)S(1)}, u32[]{:S(2)}, u32[]{:S(2)}) %collective-permute-start.1) | collective-permute-done | bytes 262176 | tf_op jit(solution)/shard_map/ppermute | solution.py:429
  31.8 2.8 %collective-permute-done.5.refs_5_.h11 = f32[2,128,256]{2,1,0:T(8,128)S(1)} collective-permute-done((f32[2,128,256]{2,1,0:T(8,128)S(1)}, f32[2,128,256]{2,1,0:T(8,128)S(1)}, u32[]{:S(2)}, u32[]{:S(2)}) %collective-permute-start.5) | collective-permute-done | bytes 262176 | tf_op jit(solution)/shard_map/ppermute | solution.py:429
  36.1 1.0 collective-permute-done.10.got_sib
  38.3 7.5 %position.1 = (f32[2,2,256,256]{3,2,1,0:T(8,128)S(1)}, f32[2,256,256]{2,1,0:T(8,128)S(1)}, f32[2,256,256]{2,1,0:T(8,128)S(1)}) custom-call(s32[9,4]{1,0:T(8,128)S(1)} %get-tuple-element.29.plan, f32[8,128]{1,0:T(8,128)S(1)} %joined.1, f32[2,2,512,512]{3,2,1,0:T(8,128)S(1)} %copy-done, f32[2,128,256]{2,1,0:T(8,128)S(1)} %tied.1.refs_0_.h00, ...), custom_call_target="tpu_custom_call" | custom-call | flops 4831838208 | bytes 16777216 | tf_op jit(solution)/shard_map/position/pallas_call | solution.py:392
  46.5 2.9 %collective-permute-done.12.y = f32[2,256,256]{2,1,0:T(8,128)S(1)} collective-permute-done((f32[2,256,256]{2,1,0:T(8,128)S(1)}, f32[2,256,256]{2,1,0:T(8,128)S(1)}, u32[]{:S(2)}, u32[]{:S(2)}) %collective-permute-start.12) | collective-permute-done | bytes 524320 | tf_op jit(solution)/shard_map/ppermute | solution.py:421
  49.5 2.2 %rows.1 = (f32[2,2,4,64,256]{4,3,2,1,0:T(8,128)}, f32[2,2,4,64,256]{4,3,2,1,0:T(8,128)S(1)}, f32[8,128]{1,0:T(8,128)S(1)}) custom-call(s32[9,4]{1,0:T(8,128)S(1)} %get-tuple-element.29.plan, f32[2,2,256,256]{3,2,1,0:T(8,128)S(1)} %get-tuple-element.34.g0, f32[2,2,256,256]{3,2,1,0:T(8,128)S(1)} %collective-permute-done.11.g1, ...), custom_call_target="tpu_custom_call" | custom-call | flops 1048576 | bytes 262144 | tf_op jit(solution)/shard_map/rows/pallas_call | solution.py:392
  52.3 21.4 %all_to_all.20.refs_0_ = f32[16,32,256]{2,1,0:T(8,128)S(1)} all-to-all(f32[16,32,256]{2,1,0:T(8,128)S(1)} %bitcast.21), channel_id=1, replica_groups=mesh['z'=8,'x'=4,'y'=4,'c'=2] {'x','y'}, dimensions={0} | all-to-all | bytes 1048576 | tf_op jit(solution)/shard_map/all_to_all | solution.py:519
  73.7 0.7 spread.2
  74.4 9.0 %all-to-all-start.2 = ((f32[8,32,256]{2,1,0:T(8,128)}), f32[8,32,256]{2,1,0:T(8,128)S(1)}, u32[]{:S(2)}, u32[]{:S(2)}) async-start(f32[8,32,256]{2,1,0:T(8,128)} %get-tuple-element.49), calls=%async_computation.2 | async-start | bytes 524288 | tf_op jit(solution)/shard_map/all_to_all | solution.py:527
  83.4 1.4 %place.1 = (f32[4,64,256]{2,1,0:T(8,128)S(1)}, f32[4,64,512]{2,1,0:T(8,128)S(1)}, f32[4,64,256]{2,1,0:T(8,128)S(1)}, f32[4,64,512]{2,1,0:T(8,128)S(1)}, f32[8,128]{1,0:T(8,128)S(1)}) custom-call(s32[9,4]{1,0:T(8,128)S(1)} %get-tuple-element.29.plan, f32[2,2,4,64,256]{4,3,2,1,0:T(8,128)S(1)} %get-tuple-element.38.kept, ...), custom_call_target="tpu_custom_call" | custom-call | flops 1048576 | bytes 262144 | tf_op jit(solution)/shard_map/place/pallas_call | solution.py:392
  84.8 1.5 %collective-permute-start.15 = (f32[4,64,256]{2,1,0:T(8,128)S(1)}, f32[4,64,256]{2,1,0:T(8,128)S(1)}, u32[]{:S(2)}, u32[]{:S(2)}) collective-permute-start(f32[4,64,256]{2,1,0:T(8,128)S(1)} %get-tuple-element.46), channel_id=1, source_target_pairs={{0,6},{1,3},{2,4},{3,1},{4,2},{5,7},{6,0},{7,5},{8,14},{9,11},{10,... | collective-permute-start | bytes 786440 | tf_op jit(solution)/shard_map/ppermute | solution.py:429
  86.3 6.2 %collective-permute-done.15.y = f32[4,64,256]{2,1,0:T(8,128)S(1)} collective-permute-done((f32[4,64,256]{2,1,0:T(8,128)S(1)}, f32[4,64,256]{2,1,0:T(8,128)S(1)}, u32[]{:S(2)}, u32[]{:S(2)}) %collective-permute-start.15) | collective-permute-done | bytes 262176 | tf_op jit(solution)/shard_map/ppermute | solution.py:429
  92.8 0.9 spread.3
  93.6 4.3 %all-to-all-start.3 = ((f32[16,32,256]{2,1,0:T(8,128)}), f32[16,32,256]{2,1,0:T(8,128)S(1)}, u32[]{:S(2)}, u32[]{:S(2)}) async-start(f32[16,32,256]{2,1,0:T(8,128)} %get-tuple-element.51), calls=%async_computation.3 | async-start | bytes 1048576 | tf_op jit(solution)/shard_map/all_to_all | solution.py:538
  97.9 3.1 %collective-permute-start.14 = (f32[4,64,512]{2,1,0:T(8,128)S(1)}, f32[4,64,512]{2,1,0:T(8,128)S(1)}, u32[]{:S(2)}, u32[]{:S(2)}) collective-permute-start(f32[4,64,512]{2,1,0:T(8,128)S(1)} %get-tuple-element.44), channel_id=1, source_target_pairs={{0,6},{1,3},{2,4},{3,1},{4,2},{5,7},{6,0},{7,5},{8,14},{9,11},{10,... | collective-permute-start | bytes 1572872 | tf_op jit(solution)/shard_map/ppermute | solution.py:429
  101.1 3.4 %collective-permute-start.16 = (f32[4,64,256]{2,1,0:T(8,128)S(1)}, f32[4,64,256]{2,1,0:T(8,128)S(1)}, u32[]{:S(2)}, u32[]{:S(2)}) collective-permute-start(f32[4,64,256]{2,1,0:T(8,128)S(1)} %get-tuple-element.48), channel_id=1, source_target_pairs={{0,8},{8,16},{16,24},{24,32},{32,40},{40,48},{48,56},{56,64},{64,7... | collective-permute-start | bytes 786440 | tf_op jit(solution)/shard_map/ppermute | solution.py:434
  104.4 9.2 %all-to-all-done.3 = f32[16,32,256]{2,1,0:T(8,128)S(1)} async-done(((f32[16,32,256]{2,1,0:T(8,128)}), f32[16,32,256]{2,1,0:T(8,128)S(1)}, u32[]{:S(2)}, u32[]{:S(2)}) %all-to-all-start.3) | async-done | bytes 524320 | tf_op jit(solution)/shard_map/all_to_all | solution.py:538
  113.8 0.9 pad_maximum_fusion.1
  114.6 0.9 collective-permute-done.17.y
  115.5 1.0 stacked.1
  (43 shorter events, 5.6 us)
Async XLA Ops:
  2.8 14.9 %collective-permute-start.8 = (f32[256,256]{1,0:T(8,128)S(1)}, f32[256,256]{1,0:T(8,128)S(1)}, u32[]{:S(2)}, u32[]{:S(2)}) collective-permute-start(f32[256,256]{1,0:T(8,128)S(1)} %get-tuple-element.57.mine_1), channel_id=1, source_target_pairs={{0,2},{1,7},{2,0},{3,5},{4,6},{5,3},{6,4},{7,1},{8,10},{9,15},{10,... | collective-permute-start | bytes 786440 | tf_op jit(solution)/shard_map/ppermute | solution.py:429
  4.5 20.8 %collective-permute-start = (f32[2,128,256]{2,1,0:T(8,128)S(1)}, f32[2,128,256]{2,1,0:T(8,128)S(1)}, u32[]{:S(2)}, u32[]{:S(2)}) collective-permute-start(f32[2,128,256]{2,1,0:T(8,128)S(1)} %get-tuple-element.30), channel_id=1, source_target_pairs={{8,0},{16,8},{24,16},{32,24},{40,32},{48,40},{56,48},{64,56},{72,6... | collective-permute-start | bytes 786440 | tf_op jit(solution)/shard_map/ppermute | solution.py:434
  8.7 17.3 %collective-permute-start.4 = (f32[2,128,256]{2,1,0:T(8,128)S(1)}, f32[2,128,256]{2,1,0:T(8,128)S(1)}, u32[]{:S(2)}, u32[]{:S(2)}) collective-permute-start(f32[2,128,256]{2,1,0:T(8,128)S(1)} %get-tuple-element.32), channel_id=1, source_target_pairs={{8,0},{16,8},{24,16},{32,24},{40,32},{48,40},{56,48},{64,56},{72,6... | collective-permute-start | bytes 786440 | tf_op jit(solution)/shard_map/ppermute | solution.py:434
  13.6 9.7 %all-to-all-start = ((s32[8,8,128]{2,1,0:T(8,128)}), s32[8,8,128]{2,1,0:T(8,128)S(1)}, u32[]{:S(2)}, u32[]{:S(2)}) async-start(s32[8,8,128]{2,1,0:T(8,128)} %broadcast_in_dim.18), calls=%async_computation | async-start | bytes 65536 | tf_op jit(solution)/shard_map/all_to_all | solution.py:479
  17.8 16.8 %collective-permute-start.9 = (f32[2,256,256]{2,1,0:T(8,128)S(1)}, f32[2,256,256]{2,1,0:T(8,128)S(1)}, u32[]{:S(2)}, u32[]{:S(2)}) collective-permute-start(f32[2,256,256]{2,1,0:T(8,128)S(1)} %pad_maximum_fusion), channel_id=1, source_target_pairs={{0,6},{1,3},{2,4},{3,1},{4,2},{5,7},{6,0},{7,5},{8,14},{9,11},{10,... | collective-permute-start | bytes 1572872 | tf_op jit(solution)/shard_map/ppermute | solution.py:429
  25.3 6.5 %collective-permute-start.1 = (f32[2,128,256]{2,1,0:T(8,128)S(1)}, f32[2,128,256]{2,1,0:T(8,128)S(1)}, u32[]{:S(2)}, u32[]{:S(2)}) collective-permute-start(f32[2,128,256]{2,1,0:T(8,128)S(1)} %tied.1.refs_0_.h00), channel_id=1, source_target_pairs={{0,2},{1,7},{2,0},{3,5},{4,6},{5,3},{6,4},{7,1},{8,10},{9,15},{10,... | collective-permute-start | bytes 786440 | tf_op jit(solution)/shard_map/ppermute | solution.py:429
  26.0 8.5 %collective-permute-start.5 = (f32[2,128,256]{2,1,0:T(8,128)S(1)}, f32[2,128,256]{2,1,0:T(8,128)S(1)}, u32[]{:S(2)}, u32[]{:S(2)}) collective-permute-start(f32[2,128,256]{2,1,0:T(8,128)S(1)} %collective-permute-done.4.refs_4_.h10), channel_id=1, source_target_pairs={{0,2},{1,7},{2,0},{3,5},{4,6},{5,3},{6,4},{7,1},{8,10},{9,15},{10,... | collective-permute-start | bytes 786440 | tf_op jit(solution)/shard_map/ppermute | solution.py:429
  27.4 8.5 %collective-permute-start.2 = (f32[2,128,256]{2,1,0:T(8,128)S(1)}, f32[2,128,256]{2,1,0:T(8,128)S(1)}, u32[]{:S(2)}, u32[]{:S(2)}) collective-permute-start(f32[2,128,256]{2,1,0:T(8,128)S(1)} %tied.1.refs_0_.h00), channel_id=1, source_target_pairs={{0,1},{1,0},{2,3},{3,2},{4,5},{5,4},{6,7},{7,6},{8,9},{9,8},{10,11... | collective-permute-start | bytes 786440 | tf_op jit(solution)/shard_map/ppermute | solution.py:421
  27.8 8.1 %collective-permute-start.6 = (f32[2,128,256]{2,1,0:T(8,128)S(1)}, f32[2,128,256]{2,1,0:T(8,128)S(1)}, u32[]{:S(2)}, u32[]{:S(2)}) collective-permute-start(f32[2,128,256]{2,1,0:T(8,128)S(1)} %collective-permute-done.4.refs_4_.h10), channel_id=1, source_target_pairs={{0,1},{1,0},{2,3},{3,2},{4,5},{5,4},{6,7},{7,6},{8,9},{9,8},{10,11... | collective-permute-start | bytes 786440 | tf_op jit(solution)/shard_map/ppermute | solution.py:421
  31.8 4.2 %collective-permute-start.3 = (f32[2,128,256]{2,1,0:T(8,128)S(1)}, f32[2,128,256]{2,1,0:T(8,128)S(1)}, u32[]{:S(2)}, u32[]{:S(2)}) collective-permute-start(f32[2,128,256]{2,1,0:T(8,128)S(1)} %collective-permute-done.1.refs_1_.h01), channel_id=1, source_target_pairs={{0,1},{1,0},{2,3},{3,2},{4,5},{5,4},{6,7},{7,6},{8,9},{9,8},{10,11... | collective-permute-start | bytes 786440 | tf_op jit(solution)/shard_map/ppermute | solution.py:421
  34.6 1.5 %collective-permute-start.7 = (f32[2,128,256]{2,1,0:T(8,128)S(1)}, f32[2,128,256]{2,1,0:T(8,128)S(1)}, u32[]{:S(2)}, u32[]{:S(2)}) collective-permute-start(f32[2,128,256]{2,1,0:T(8,128)S(1)} %collective-permute-done.5.refs_5_.h11), channel_id=1, source_target_pairs={{0,1},{1,0},{2,3},{3,2},{4,5},{5,4},{6,7},{7,6},{8,9},{9,8},{10,11... | collective-permute-start | bytes 786440 | tf_op jit(solution)/shard_map/ppermute | solution.py:421
  35.3 2.2 %copy-start = (f32[2,2,512,512]{3,2,1,0:T(8,128)S(1)}, f32[2,2,512,512]{3,2,1,0:T(8,128)}, u32[]{:S(2)}) copy-start(f32[2,2,512,512]{3,2,1,0:T(8,128)} %strip.1) | copy-start | bytes 12582916
  35.3 2.5 %copy-start.1 = (f32[2,2,256,256]{3,2,1,0:T(8,128)S(1)}, f32[2,2,256,256]{3,2,1,0:T(8,128)}, u32[]{:S(2)}) copy-start(f32[2,2,256,256]{3,2,1,0:T(8,128)} %probe.1) | copy-start | bytes 3145732
  35.3 2.8 %copy-start.2 = (bf16[9,256,256]{2,1,0:T(8,128)(2,1)S(1)}, bf16[9,256,256]{2,1,0:T(8,128)(2,1)}, u32[]{:S(2)}) copy-start(bf16[9,256,256]{2,1,0:T(8,128)(2,1)} %constant.27.clone.tables) | copy-start | bytes 3538948
  35.3 2.9 %copy-start.3 = (f32[2,256,256]{2,1,0:T(8,128)S(1)}, f32[2,256,256]{2,1,0:T(8,128)}, u32[]{:S(2)}) copy-start(f32[2,256,256]{2,1,0:T(8,128)} %constant.28.clone.transfer) | copy-start | bytes 1572868
  35.3 1.8 %collective-permute-start.10 = (f32[256,256]{1,0:T(8,128)S(1)}, f32[256,256]{1,0:T(8,128)S(1)}, u32[]{:S(2)}, u32[]{:S(2)}) collective-permute-start(f32[256,256]{1,0:T(8,128)S(1)} %pick.1), channel_id=1, source_target_pairs={{0,1},{1,0},{2,3},{3,2},{4,5},{5,4},{6,7},{7,6},{8,9},{9,8},{10,11... | collective-permute-start | bytes 786440 | tf_op jit(solution)/shard_map/ppermute | solution.py:421
  45.8 3.7 %collective-permute-start.11 = (f32[2,2,256,256]{3,2,1,0:T(8,128)S(1)}, f32[2,2,256,256]{3,2,1,0:T(8,128)S(1)}, u32[]{:S(2)}, u32[]{:S(2)}) collective-permute-start(f32[2,2,256,256]{3,2,1,0:T(8,128)S(1)} %get-tuple-element.34.g0), channel_id=1, source_target_pairs={{0,1},{1,0},{2,3},{3,2},{4,5},{5,4},{6,7},{7,6},{8,9},{9,8},{10,11... | collective-permute-start | bytes 3145736 | tf_op jit(solution)/shard_map/ppermute | solution.py:421
  46.4 3.0 %collective-permute-start.12 = (f32[2,256,256]{2,1,0:T(8,128)S(1)}, f32[2,256,256]{2,1,0:T(8,128)S(1)}, u32[]{:S(2)}, u32[]{:S(2)}) collective-permute-start(f32[2,256,256]{2,1,0:T(8,128)S(1)} %get-tuple-element.36), channel_id=1, source_target_pairs={{0,1},{1,0},{2,3},{3,2},{4,5},{5,4},{6,7},{7,6},{8,9},{9,8},{10,11... | collective-permute-start | bytes 1572872 | tf_op jit(solution)/shard_map/ppermute | solution.py:421
  51.7 31.7 %collective-permute-start.13 = (f32[2,2,4,64,256]{4,3,2,1,0:T(8,128)}, f32[2,2,4,64,256]{4,3,2,1,0:T(8,128)S(1)}, u32[]{:S(2)}, u32[]{:S(2)}) collective-permute-start(f32[2,2,4,64,256]{4,3,2,1,0:T(8,128)} %get-tuple-element.39), channel_id=1, source_target_pairs={{0,2},{1,7},{2,0},{3,5},{4,6},{5,3},{6,4},{7,1},{8,10},{9,15},{10,... | collective-permute-start | bytes 3145736 | tf_op jit(solution)/shard_map/ppermute | solution.py:429
  74.4 18.4 %all-to-all-start.2 = ((f32[8,32,256]{2,1,0:T(8,128)}), f32[8,32,256]{2,1,0:T(8,128)S(1)}, u32[]{:S(2)}, u32[]{:S(2)}) async-start(f32[8,32,256]{2,1,0:T(8,128)} %get-tuple-element.49), calls=%async_computation.2 | async-start | bytes 524288 | tf_op jit(solution)/shard_map/all_to_all | solution.py:527
  84.8 7.7 %collective-permute-start.15 = (f32[4,64,256]{2,1,0:T(8,128)S(1)}, f32[4,64,256]{2,1,0:T(8,128)S(1)}, u32[]{:S(2)}, u32[]{:S(2)}) collective-permute-start(f32[4,64,256]{2,1,0:T(8,128)S(1)} %get-tuple-element.46), channel_id=1, source_target_pairs={{0,6},{1,3},{2,4},{3,1},{4,2},{5,7},{6,0},{7,5},{8,14},{9,11},{10,... | collective-permute-start | bytes 786440 | tf_op jit(solution)/shard_map/ppermute | solution.py:429
  93.6 20.0 %all-to-all-start.3 = ((f32[16,32,256]{2,1,0:T(8,128)}), f32[16,32,256]{2,1,0:T(8,128)S(1)}, u32[]{:S(2)}, u32[]{:S(2)}) async-start(f32[16,32,256]{2,1,0:T(8,128)} %get-tuple-element.51), calls=%async_computation.3 | async-start | bytes 1048576 | tf_op jit(solution)/shard_map/all_to_all | solution.py:538
  97.9 15.7 %collective-permute-start.14 = (f32[4,64,512]{2,1,0:T(8,128)S(1)}, f32[4,64,512]{2,1,0:T(8,128)S(1)}, u32[]{:S(2)}, u32[]{:S(2)}) collective-permute-start(f32[4,64,512]{2,1,0:T(8,128)S(1)} %get-tuple-element.44), channel_id=1, source_target_pairs={{0,6},{1,3},{2,4},{3,1},{4,2},{5,7},{6,0},{7,5},{8,14},{9,11},{10,... | collective-permute-start | bytes 1572872 | tf_op jit(solution)/shard_map/ppermute | solution.py:429
  101.1 12.7 %collective-permute-start.16 = (f32[4,64,256]{2,1,0:T(8,128)S(1)}, f32[4,64,256]{2,1,0:T(8,128)S(1)}, u32[]{:S(2)}, u32[]{:S(2)}) collective-permute-start(f32[4,64,256]{2,1,0:T(8,128)S(1)} %get-tuple-element.48), channel_id=1, source_target_pairs={{0,8},{8,16},{16,24},{24,32},{32,40},{40,48},{48,56},{56,64},{64,7... | collective-permute-start | bytes 786440 | tf_op jit(solution)/shard_map/ppermute | solution.py:434
  113.6 1.9 %collective-permute-start.17 = (f32[2,256,256]{2,1,0:T(8,128)S(1)}, f32[2,256,256]{2,1,0:T(8,128)S(1)}, u32[]{:S(2)}, u32[]{:S(2)}) collective-permute-start(f32[2,256,256]{2,1,0:T(8,128)S(1)} %bitcast.19), channel_id=1, source_target_pairs={{0,1},{1,0},{2,3},{3,2},{4,5},{5,4},{6,7},{7,6},{8,9},{9,8},{10,11... | collective-permute-start | bytes 1572872 | tf_op jit(solution)/shard_map/ppermute | solution.py:421

commit v3 on v2

--- a/solution.py
+++ b/solution.py
@@ -131,12 +131,56 @@
     return pl.multiple_of(row, 8), pl.multiple_of(col, 128), r - row, c - col
 
 
+def rows_down(x, by):
+    rows, cols = x.shape
+    turned = pltpu.roll(x.reshape(rows // 8, 8, cols), by, 1)
+    none = jnp.zeros((1, 8, cols), F32)
+    above, here = jnp.concatenate([none, turned], 0), jnp.concatenate([turned, none], 0)
+    row = lax.broadcasted_iota(jnp.int32, here.shape, 1)
+    return jnp.where(row < by, above, here).reshape(rows + 8, cols)
+
+
+def rows_up(x, by):
+    rows, cols = x.shape
+    turned = pltpu.roll(x.reshape(rows // 8, 8, cols), lax.rem(8 - by, 8), 1)
+    row = lax.broadcasted_iota(jnp.int32, (rows // 8 - 1, 8, cols), 1)
+    return jnp.where(row < 8 - by, turned[:-1], turned[1:]).reshape(rows - 8, cols)
+
+
+def cols_right(x, by):
+    rows, cols = x.shape
+    blocks = [pltpu.roll(x[:, k : k + 128], by, 1) for k in range(0, cols, 128)]
+    none = jnp.zeros((rows, 128), F32)
+    col = lax.broadcasted_iota(jnp.int32, (rows, 128), 1)
+    pairs_of = zip([none] + blocks, blocks + [none])
+    return jnp.concatenate([jnp.where(col < by, a, b) for a, b in pairs_of], 1)
+
+
+def cols_left(x, by):
+    rows, cols = x.shape
+    turn = lax.rem(128 - by, 128)
+    blocks = [pltpu.roll(x[:, k : k + 128], turn, 1) for k in range(0, cols, 128)]
+    col = lax.broadcasted_iota(jnp.int32, (rows, 128), 1)
+    pairs_of = zip(blocks[:-1], blocks[1:])
+    return jnp.concatenate([jnp.where(col < 128 - by, a, b) for a, b in pairs_of], 1)
+
+
 def partners(y, c):
     near, far = jnp.bitwise_xor(y, 1), 3 - y
     return jnp.where(c == 0, near, far), jnp.where(c == 0, far, near), 3 - near
 
 
-def plan_kernel(info, me, plan, token):
+def row_kernel(counts, offsets, place, out):
+    lane = lax.broadcasted_iota(jnp.int32, out.shape, 2)
+    values = [counts[0, 0]]
+    values += [offsets[0, 0, slot, k] for slot in range(2) for k in range(2)]
+    row = jnp.zeros(out.shape, jnp.int32)
+    for k, value in enumerate(values):
+        row = jnp.where(lane == k, value, row)
+    out[...] = row
+
+
+def plan_kernel(info, me, plan):
     count = [info[s, 0, 0] for s in range(8)]
     zeros, doubles = jnp.int32(0), jnp.int32(0)
     zero_rank, double_rank = [], []
@@ -157,27 +201,8 @@
         plan[s, 1] = slot
         plan[s, 2] = info[source, 0, 1 + 2 * slot]
         plan[s, 3] = info[source, 0, 2 + 2 * slot]
-    token[...] = jnp.zeros_like(token)
-    plan[8, 0] = me[0, 5]
-    plan[8, 1] = me[0, 6]
-
-
-def pick_kernel(plan, mine_1, got_a, got_b, for_sib, sem):
-    y, c = plan[8, 0], plan[8, 1]
-    source = plan[2 * y + 1 - c, 0]
-    a, b, e = partners(y, c)
-
-    def give(device, ref):
-        @pl.when(source == device)
-        def _():
-            copy = pltpu.make_async_copy(ref, for_sib, sem)
-            copy.start()
-            copy.wait()
-
-    give(2 * y + c, mine_1)
-    give(2 * a + c, got_a)
-    give(2 * b + c, got_b.at[0])
-    give(2 * e + c, got_b.at[1])
+    plan[8, 0] = me[0]
+    plan[8, 1] = me[1]
 
 
 def tie_kernel(*refs):
@@ -190,7 +215,7 @@
 
 def compute_kernel(
     plan, joined, strip, h00, h01, h02, h03, h10, h11, h12, h13, probe,
-    mine_0, mine_1, got_a, got_b, got_sib, tables, transfer,
+    mine_0, mine_1, got_a, got_b, sib_1, sib_a, sib_b, tables, transfer,
     grad, mine, sib, halo, full, obj, us, psi, meas, sem,
 ):
     y, c = plan[8, 0], plan[8, 1]
@@ -203,13 +228,17 @@
     core = lax.rem(source, 2)
     chip = lax.div(source, 2)
     here = jnp.logical_and(slot == 1, core == c)
+    there = jnp.logical_and(slot == 1, core != c)
     choices = [
         (slot == 0, mine_0),
         (jnp.logical_and(here, chip == y), mine_1),
         (jnp.logical_and(here, chip == a), got_a),
         (jnp.logical_and(here, chip == b), got_b.at[0]),
         (jnp.logical_and(here, chip == e), got_b.at[1]),
-        (jnp.logical_and(slot == 1, core != c), got_sib),
+        (jnp.logical_and(there, chip == y), sib_1),
+        (jnp.logical_and(there, chip == b), sib_a),
+        (jnp.logical_and(there, chip == a), sib_b.at[0]),
+        (jnp.logical_and(there, chip == e), sib_b.at[1]),
     ]
     for chosen, ref in choices:
 
@@ -238,9 +267,7 @@
 
     def window(layer):
         for part in range(2):
-            x = pltpu.roll(full[part, layer], lax.rem(384 - dc, 384), 1)[:, :256]
-            x = pltpu.roll(x, lax.rem(264 - dr, 264), 0)
-            obj[layer, part] = x[:256]
+            obj[layer, part] = rows_up(cols_left(full[part, layer], dc), dr)
 
     def load(ref, *index):
         return ref[(*index, 0)], ref[(*index, 1)]
@@ -311,22 +338,18 @@
 def rows_kernel(plan, g0, g1, before, msg, kept, token, tall):
     y, c = plan[8, 0], plan[8, 1]
     a, b, e = partners(y, c)
-    tall[:, :72] = jnp.zeros((4, 72, 256), F32)
-    tall[:, 328:] = jnp.zeros((4, 72, 256), F32)
+    tall[:, :64] = jnp.zeros((4, 64, 256), F32)
+    tall[:, 328:] = jnp.zeros((4, 64, 256), F32)
     for w, g in enumerate((g0, g1)):
         core = c if w == 0 else 1 - c
         r = plan[2 * y + core, 2]
+        dr = lax.rem(r, 8)
         for plane in range(4):
-            tall[plane, 72:328] = g[plane // 2, plane % 2]
+            tall[plane, 64:328] = rows_down(g[plane // 2, plane % 2], dr)
 
         def put(out, chip):
-            start = jnp.clip(72 + 128 * chip + 64 * c - r, 0, 328)
-            row = lax.div(start, 8) * 8
-            shift = start - row
-            row = pl.multiple_of(row, 8)
-            for plane in range(4):
-                x = pltpu.roll(tall[plane, pl.ds(row, 72), :], lax.rem(72 - shift, 72), 0)
-                out[plane] = x[:64]
+            start = jnp.clip(64 + 128 * chip + 64 * c - (r - dr), 0, 328)
+            out[...] = tall[:, pl.ds(pl.multiple_of(start, 8), 64), :]
 
         put(msg.at[w, 0], a)
         put(msg.at[w, 1], e)
@@ -348,8 +371,7 @@
         _, col, _, dc = corner_of(jnp.int32(0), plan[2 * chip + core, 3], 512)
         for d in range(2):
             for plane in range(4):
-                x = jnp.concatenate([ref[w, d, plane], jnp.zeros((64, 128), F32)], 1)
-                acc[d, plane, :, pl.ds(col, 384)] += pltpu.roll(x, dc, 1)
+                acc[d, plane, :, pl.ds(col, 384)] += cols_right(ref[w, d, plane], dc)
     keep_strip[...] = acc[0, :, :, :512]
     keep_edge[...] = acc[0, :, :, 512:]
     send_strip[...] = acc[1, :, :, :512]
@@ -408,7 +430,7 @@
         in_specs=[VMEM] * (1 + len(others)),
         out_specs=VMEM,
         input_output_aliases={0: 0},
-        compiler_params=pltpu.CompilerParams(vmem_limit_bytes=4 << 20),
+        compiler_params=pltpu.CompilerParams(vmem_limit_bytes=16 << 20),
         name="tied",
     )(x, *others)
 
@@ -474,39 +496,36 @@
     )
     halos = [tile_shift(part, -1) for part in parts]
 
-    own_row = jnp.concatenate([counts.reshape(1), offsets.reshape(4), y[None], c[None]])
-    own_row = jnp.pad(own_row, (0, 121))
-    info = lax.all_to_all(jnp.broadcast_to(own_row, (8, 8, 128)), ("y", "c"), 0, 0, tiled=True)
-    own_row = jnp.broadcast_to(own_row, (8, 128))
+    place = jnp.stack([y, c])
+    own_row = run_kernel(
+        row_kernel, "row", (counts, offsets, place), [SMEM] * 3,
+        jax.ShapeDtypeStruct((8, 1, 128), jnp.int32), VMEM, [], 1 << 10, 4,
+    )
+    info = lax.all_to_all(own_row, ("y", "c"), 0, 0, tiled=True)
 
     mine_0, mine_1 = measured[0, 0, 0], measured[0, 0, 1]
-    got_a = y_swap(mine_1, True)
+    tables, transfer = jnp.asarray(tables), jnp.asarray(transfer)
+    got_a = tied(y_swap(mine_1, True), own_row)
     got_b = y_swap(jnp.stack([mine_1, got_a]), False)
-    plan, planned = run_kernel(
-        plan_kernel, "plan", (info, own_row), [SMEM] * 2,
-        [jax.ShapeDtypeStruct((9, 4), jnp.int32), struct(8, 128)], [SMEM, VMEM],
-        [], 1 << 20, 4,
-    )
-    for_sib = run_kernel(
-        pick_kernel, "pick", (plan, mine_1, got_a, got_b), [SMEM, ANY, ANY, ANY],
-        struct(n, n), ANY, [pltpu.SemaphoreType.DMA(())], 1 << 20, 4,
-    )
-    got_sib = core_swap(for_sib)
+    plan = run_kernel(
+        plan_kernel, "plan", (info, place), [SMEM] * 2,
+        jax.ShapeDtypeStruct((9, 4), jnp.int32), SMEM, [], 1 << 33, 4,
+    )
+    sib_maps = [core_swap(x) for x in (mine_1, got_a, got_b)]
 
     pieces = []
-    halos[0] = tied(halos[0], planned)
     for got in halos:
         other = y_swap(got, True)
         pieces += [got, other, core_swap(got), core_swap(other)]
 
     joined = run_kernel(
-        join_kernel, "joined", tuple(pieces), [ANY] * 8, struct(8, 128), VMEM, [], LONG, 4,
+        join_kernel, "joined", (*pieces, *sib_maps), [ANY] * 11, struct(8, 128), VMEM, [], LONG, 4,
     )
     grad, mine, sib = run_kernel(
         compute_kernel, "position",
-        (plan, joined, object_field, *pieces, probe, mine_0, mine_1, got_a, got_b, got_sib,
-         jnp.asarray(tables), jnp.asarray(transfer)),
-        [SMEM] + [VMEM] * 11 + [ANY] * 5 + [VMEM] * 2,
+        (plan, joined, object_field, *pieces, probe, mine_0, mine_1, got_a, got_b, *sib_maps,
+         tables, transfer),
+        [SMEM] + [VMEM] * 11 + [ANY] * 7 + [VMEM] * 2,
         [struct(2, 2, n, n), struct(2, n, n), struct(2, n, n)], [VMEM] * 3,
         [pltpu.VMEM((2, 2, 512, n), F32), pltpu.VMEM((2, 2, 264, 384), F32)]
         + [pltpu.VMEM((2, 2, n, n), F32)] * 3
@@ -519,7 +538,7 @@
     pieces_1 = lax.all_to_all(total.reshape(16, 32, n), ("x", "y"), 0, 0, tiled=True)
     msg, kept, token = run_kernel(
         rows_kernel, "rows", (plan, grad, grad_sib, token), [SMEM, VMEM, VMEM, VMEM],
-        [struct(2, 2, 4, 64, n)] * 2 + [TOKEN], [VMEM] * 3, [pltpu.VMEM((4, 400, n), F32)],
+        [struct(2, 2, 4, 64, n)] * 2 + [TOKEN], [VMEM] * 3, [pltpu.VMEM((4, 392, n), F32)],
         1 << 20, 12,
     )
     got = y_swap(msg, True)

time: 117 us -> 116 us (level)
  waiting for transfers between devices: 29.5 us -> 25.3 us
    ppermute x7, waiting for transfers between devices: 12.8 us -> 8.78 us  [y_swap(): return lax.ppermute(x, ('y', 'c'), pairs(8, partner))]
    ppermute x3, waiting for transfers between devices: 0.01 us -> 2.96 us  [tile_shift(): lax.ppermute(x, ('z', 'x'), [(i, i + by) for i in range(n) if 0 <= i + by...]
    ppermute x7, starting transfers between devices: 12.3 us -> 9.47 us  [y_swap(): return lax.ppermute(x, ('y', 'c'), pairs(8, partner))]
    ppermute x8 -> x10, starting transfers between devices: 1.76 us -> 4.2 us  [core_swap(): return lax.ppermute(x, 'c', [(0, 1), (1, 0)])]
    all_to_all x1, waiting for transfers between devices: 2.19 us -> 0.05 us  [shards(): info = lax.all_to_all(own_row, ('y', 'c'), 0, 0, tiled=True)]
    unnamed x8 -> x10, local copies, waits for them, and re-layouts: 1.17 us -> 3.25 us
    all_to_all x1, starting transfers between devices: 4.29 us -> 5.84 us  [shards(): lax.all_to_all(spread_2, ('x', 'y'), 0, 0, tiled=True).reshape(2, n, n)]
    ppermute x8 -> x10, waiting for transfers between devices: 4.99 us -> 4.16 us  [core_swap(): return lax.ppermute(x, 'c', [(0, 1), (1, 0)])]
  transfers between devices with their start and end apart: 21 -> 23, of which waited for: 10 -> 10; matrix products, arithmetic and copies ran while one was open for 2% -> 1% of each run, Pallas kernels for 4% -> 5%
where the time goes in v3:
time: 116 us; the launch traced here: 115 us
  starting transfers between devices  42.7 us (37%)
  waiting for transfers between devices  25.3 us (22%)
  blocking collectives  21.9 us (19%)
  Pallas kernels  17.2 us (15%)
  local copies, waits for them, and re-layouts  5.41 us (5%)
  between operations  1.47 us (1%)
    all_to_all x1, blocking collectives, shards(): lax.all_to_all(total.reshape(16, 32, n), ('x', 'y'), 0, 0, tiled=True)  21.9 us
    pallas_call x11, Pallas kernels, run_kernel(): pl.pallas_call(body, out_shape=outs, in_specs=in_specs, out_specs=out_spe...  16.5 us
    ppermute x3, starting transfers between devices, tile_shift(): lax.ppermute(x, ('z', 'x'), [(i, i + by) for i in range(n) if 0 <= i + by...  10.3 us
    ppermute x7, starting transfers between devices, y_swap(): return lax.ppermute(x, ('y', 'c'), pairs(8, partner))  9.47 us
    all_to_all x1, waiting for transfers between devices, shards(): lax.all_to_all(spread_2, ('x', 'y'), 0, 0, tiled=True).reshape(2, n, n)  9.21 us
    all_to_all x1, starting transfers between devices, shards(): pieces_2 = lax.all_to_all(spread_1, 'z', 0, 0, tiled=True)  9.05 us
    ppermute x7, waiting for transfers between devices, y_swap(): return lax.ppermute(x, ('y', 'c'), pairs(8, partner))  8.78 us
    all_to_all x1, starting transfers between devices, shards(): lax.all_to_all(spread_2, ('x', 'y'), 0, 0, tiled=True).reshape(2, n, n)  5.84 us
  transfers between devices with their start and end apart: 23, of which 10 were waited for; matrix products, arithmetic and copies ran while one was open for 1% of the time, Pallas kernels for 5%

profile of v3, /device:TPU:32, one launch (start us, length us, event | category | flops | bytes accessed | tf_op | source)
XLA Modules:
  0.0 115.1 jit_solution(16950580492832618709)
XLA Ops:
  0.6 1.1 dynamic-slice_bitcast_fusion
  1.7 1.1 slice_bitcast_fusion
  2.8 1.7 %collective-permute-start.9 = (f32[256,256]{1,0:T(8,128)S(1)}, f32[256,256]{1,0:T(8,128)S(1)}, u32[]{:S(2)}, u32[]{:S(2)}) collective-permute-start(f32[256,256]{1,0:T(8,128)S(1)} %get-tuple-element.54.mine_1), channel_id=1, source_target_pairs={{0,2},{1,7},{2,0},{3,5},{4,6},{5,3},{6,4},{7,1},{8,10},{9,15},{10,... | collective-permute-start | bytes 786440 | tf_op jit(solution)/shard_map/ppermute | solution.py:451
  4.5 4.2 %collective-permute-start = (f32[2,128,256]{2,1,0:T(8,128)S(1)}, f32[2,128,256]{2,1,0:T(8,128)S(1)}, u32[]{:S(2)}, u32[]{:S(2)}) collective-permute-start(f32[2,128,256]{2,1,0:T(8,128)S(1)} %get-tuple-element.27), channel_id=1, source_target_pairs={{8,0},{16,8},{24,16},{32,24},{40,32},{48,40},{56,48},{64,56},{72,6... | collective-permute-start | bytes 786440 | tf_op jit(solution)/shard_map/ppermute | solution.py:456
  8.7 2.7 %collective-permute-start.4 = (f32[2,128,256]{2,1,0:T(8,128)S(1)}, f32[2,128,256]{2,1,0:T(8,128)S(1)}, u32[]{:S(2)}, u32[]{:S(2)}) collective-permute-start(f32[2,128,256]{2,1,0:T(8,128)S(1)} %get-tuple-element.28), channel_id=1, source_target_pairs={{8,0},{16,8},{24,16},{32,24},{40,32},{48,40},{56,48},{64,56},{72,6... | collective-permute-start | bytes 786440 | tf_op jit(solution)/shard_map/ppermute | solution.py:456
  12.8 1.2 row.1.refs_1_
  14.0 0.7 tied.1.got_a
  14.7 2.3 %collective-permute-start.11 = (f32[2,256,256]{2,1,0:T(8,128)S(1)}, f32[2,256,256]{2,1,0:T(8,128)S(1)}, u32[]{:S(2)}, u32[]{:S(2)}) collective-permute-start(f32[2,256,256]{2,1,0:T(8,128)S(1)} %pad_maximum_fusion), channel_id=1, source_target_pairs={{0,6},{1,3},{2,4},{3,1},{4,2},{5,7},{6,0},{7,5},{8,14},{9,11},{10,... | collective-permute-start | bytes 1572872 | tf_op jit(solution)/shard_map/ppermute | solution.py:451
  18.2 3.0 %collective-permute-done.4.refs_4_.h10 = f32[2,128,256]{2,1,0:T(8,128)S(1)} collective-permute-done((f32[2,128,256]{2,1,0:T(8,128)S(1)}, f32[2,128,256]{2,1,0:T(8,128)S(1)}, u32[]{:S(2)}, u32[]{:S(2)}) %collective-permute-start.4) | collective-permute-done | bytes 262176 | tf_op jit(solution)/shard_map/ppermute | solution.py:456
  21.3 3.8 %all-to-all-start = ((s32[8,1,128]{2,1,0:T(1,128)}), s32[8,1,128]{2,1,0:T(1,128)S(1)}, u32[]{:S(2)}, u32[]{:S(2)}) async-start(s32[8,1,128]{2,1,0:T(1,128)} %row.1.refs_1_), calls=%async_computation | async-start | bytes 8192 | tf_op jit(solution)/shard_map/all_to_all | solution.py:504
  26.3 0.8 collective-permute-start.3
  27.1 2.1 %collective-permute-done.5.refs_5_.h11 = f32[2,128,256]{2,1,0:T(8,128)} collective-permute-done((f32[2,128,256]{2,1,0:T(8,128)S(1)}, f32[2,128,256]{2,1,0:T(8,128)}, u32[]{:S(2)}, u32[]{:S(2)}) %collective-permute-start.5) | collective-permute-done | bytes 262176 | tf_op jit(solution)/shard_map/ppermute | solution.py:451
  29.2 1.6 %collective-permute-start.7 = (f32[2,128,256]{2,1,0:T(8,128)}, f32[2,128,256]{2,1,0:T(8,128)}, u32[]{:S(2)}, u32[]{:S(2)}) collective-permute-start(f32[2,128,256]{2,1,0:T(8,128)} %collective-permute-done.5.refs_5_.h11), channel_id=1, source_target_pairs={{0,1},{1,0},{2,3},{3,2},{4,5},{5,4},{6,7},{7,6},{8,9},{9,8},{10,11... | collective-permute-start | bytes 786440 | tf_op jit(solution)/shard_map/ppermute | solution.py:443
  30.8 1.4 %plan.1 = s32[9,4]{1,0:T(8,128)S(1)} custom-call(s32[8,1,128]{2,1,0:T(1,128)S(1)} %all-to-all-done.info, s32[2]{0:T(128)S(1)} %pad_add_fusion.place.me), custom_call_target="tpu_custom_call" | custom-call | flops 8589934592 | bytes 262144 | tf_op jit(solution)/shard_map/plan/pallas_call | solution.py:414
  32.7 1.8 %copy-done = f32[2,2,512,512]{3,2,1,0:T(8,128)S(1)} copy-done((f32[2,2,512,512]{3,2,1,0:T(8,128)S(1)}, f32[2,2,512,512]{3,2,1,0:T(8,128)}, u32[]{:S(2)}) %copy-start) | copy-done | bytes 4194328
  35.2 7.7 %position.1 = (f32[2,2,256,256]{3,2,1,0:T(8,128)S(1)}, f32[2,256,256]{2,1,0:T(8,128)S(1)}, f32[2,256,256]{2,1,0:T(8,128)S(1)}) custom-call(s32[9,4]{1,0:T(8,128)S(1)} %plan.1, f32[8,128]{1,0:T(8,128)S(1)} %joined.1, f32[2,2,512,512]{3,2,1,0:T(8,128)S(1)} %copy-done, f32[2,128,256]{2,1,0:T(8,128)S(1)} %collective-permute-done.refs_0_.h00, ...), custom_call_target="tpu_custom_call" | custom-call | flops 4831838208 | bytes 16777216 | tf_op jit(solution)/shard_map/position/pallas_call | solution.py:414
  43.6 2.9 %collective-permute-done.14.y = f32[2,256,256]{2,1,0:T(8,128)S(1)} collective-permute-done((f32[2,256,256]{2,1,0:T(8,128)S(1)}, f32[2,256,256]{2,1,0:T(8,128)S(1)}, u32[]{:S(2)}, u32[]{:S(2)}) %collective-permute-start.14) | collective-permute-done | bytes 524320 | tf_op jit(solution)/shard_map/ppermute | solution.py:443
  46.7 2.0 %rows.1 = (f32[2,2,4,64,256]{4,3,2,1,0:T(8,128)}, f32[2,2,4,64,256]{4,3,2,1,0:T(8,128)S(1)}, f32[8,128]{1,0:T(8,128)S(1)}) custom-call(s32[9,4]{1,0:T(8,128)S(1)} %plan.1, f32[2,2,256,256]{3,2,1,0:T(8,128)S(1)} %get-tuple-element.30.g0, f32[2,2,256,256]{3,2,1,0:T(8,128)S(1)} %collective-permute-done.13.g1, f32[8,128]{1,0:T(8,128)S(1)} %get-tuple-element.33.before), custom_call_target="tpu_custom_call" | custom-call | flops 1048576 | bytes 262144 | tf_op jit(solution)/shard_map/rows/pallas_call | solution.py:414
  48.7 21.9 %all_to_all.20.refs_0_ = f32[16,32,256]{2,1,0:T(8,128)S(1)} all-to-all(f32[16,32,256]{2,1,0:T(8,128)S(1)} %bitcast.19), channel_id=1, replica_groups=mesh['z'=8,'x'=4,'y'=4,'c'=2] {'x','y'}, dimensions={0} | all-to-all | bytes 1048576 | tf_op jit(solution)/shard_map/all_to_all | solution.py:538
  70.6 0.7 spread.2
  71.4 9.1 %all-to-all-start.2 = ((f32[8,32,256]{2,1,0:T(8,128)}), f32[8,32,256]{2,1,0:T(8,128)S(1)}, u32[]{:S(2)}, u32[]{:S(2)}) async-start(f32[8,32,256]{2,1,0:T(8,128)} %get-tuple-element.45), calls=%async_computation.2 | async-start | bytes 524288 | tf_op jit(solution)/shard_map/all_to_all | solution.py:546
  80.4 1.4 %place.1 = (f32[4,64,256]{2,1,0:T(8,128)S(1)}, f32[4,64,512]{2,1,0:T(8,128)S(1)}, f32[4,64,256]{2,1,0:T(8,128)S(1)}, f32[4,64,512]{2,1,0:T(8,128)S(1)}, f32[8,128]{1,0:T(8,128)S(1)}) custom-call(s32[9,4]{1,0:T(8,128)S(1)} %plan.1, f32[2,2,4,64,256]{4,3,2,1,0:T(8,128)S(1)} %get-tuple-element.34.kept, f32[2,2,4,64,256]{4,3,2,1,0:T(8,128)S(1)} %collective-permute-done.15.got, ...), custom_call_target="tpu_custom_call" | custom-call | flops 1048576 | bytes 262144 | tf_op jit(solution)/shard_map/place/pallas_call | solution.py:414
  81.9 1.5 %collective-permute-start.17 = (f32[4,64,256]{2,1,0:T(8,128)S(1)}, f32[4,64,256]{2,1,0:T(8,128)S(1)}, u32[]{:S(2)}, u32[]{:S(2)}) collective-permute-start(f32[4,64,256]{2,1,0:T(8,128)S(1)} %get-tuple-element.42), channel_id=1, source_target_pairs={{0,6},{1,3},{2,4},{3,1},{4,2},{5,7},{6,0},{7,5},{8,14},{9,11},{10,... | collective-permute-start | bytes 786440 | tf_op jit(solution)/shard_map/ppermute | solution.py:451
  83.4 6.2 %collective-permute-done.17.y = f32[4,64,256]{2,1,0:T(8,128)S(1)} collective-permute-done((f32[4,64,256]{2,1,0:T(8,128)S(1)}, f32[4,64,256]{2,1,0:T(8,128)S(1)}, u32[]{:S(2)}, u32[]{:S(2)}) %collective-permute-start.17) | collective-permute-done | bytes 262176 | tf_op jit(solution)/shard_map/ppermute | solution.py:451
  89.7 0.9 spread.3
  90.6 5.8 %all-to-all-start.3 = ((f32[16,32,256]{2,1,0:T(8,128)}), f32[16,32,256]{2,1,0:T(8,128)S(1)}, u32[]{:S(2)}, u32[]{:S(2)}) async-start(f32[16,32,256]{2,1,0:T(8,128)} %get-tuple-element.47), calls=%async_computation.3 | async-start | bytes 1048576 | tf_op jit(solution)/shard_map/all_to_all | solution.py:557
  96.4 3.1 %collective-permute-start.16 = (f32[4,64,512]{2,1,0:T(8,128)S(1)}, f32[4,64,512]{2,1,0:T(8,128)S(1)}, u32[]{:S(2)}, u32[]{:S(2)}) collective-permute-start(f32[4,64,512]{2,1,0:T(8,128)S(1)} %get-tuple-element.40), channel_id=1, source_target_pairs={{0,6},{1,3},{2,4},{3,1},{4,2},{5,7},{6,0},{7,5},{8,14},{9,11},{10,... | collective-permute-start | bytes 1572872 | tf_op jit(solution)/shard_map/ppermute | solution.py:451
  99.6 3.4 %collective-permute-start.18 = (f32[4,64,256]{2,1,0:T(8,128)S(1)}, f32[4,64,256]{2,1,0:T(8,128)S(1)}, u32[]{:S(2)}, u32[]{:S(2)}) collective-permute-start(f32[4,64,256]{2,1,0:T(8,128)S(1)} %get-tuple-element.44), channel_id=1, source_target_pairs={{0,8},{8,16},{16,24},{24,32},{32,40},{40,48},{48,56},{56,64},{64,7... | collective-permute-start | bytes 786440 | tf_op jit(solution)/shard_map/ppermute | solution.py:456
  103.0 9.2 %all-to-all-done.3 = f32[16,32,256]{2,1,0:T(8,128)S(1)} async-done(((f32[16,32,256]{2,1,0:T(8,128)}), f32[16,32,256]{2,1,0:T(8,128)S(1)}, u32[]{:S(2)}, u32[]{:S(2)}) %all-to-all-start.3) | async-done | bytes 524320 | tf_op jit(solution)/shard_map/all_to_all | solution.py:557
  112.3 0.9 pad_maximum_fusion.1
  113.2 0.9 collective-permute-done.19.y
  114.1 1.0 stacked.1
  (45 shorter events, 5.6 us)
Async XLA Ops:
  2.8 11.2 %collective-permute-start.9 = (f32[256,256]{1,0:T(8,128)S(1)}, f32[256,256]{1,0:T(8,128)S(1)}, u32[]{:S(2)}, u32[]{:S(2)}) collective-permute-start(f32[256,256]{1,0:T(8,128)S(1)} %get-tuple-element.54.mine_1), channel_id=1, source_target_pairs={{0,2},{1,7},{2,0},{3,5},{4,6},{5,3},{6,4},{7,1},{8,10},{9,15},{10,... | collective-permute-start | bytes 786440 | tf_op jit(solution)/shard_map/ppermute | solution.py:451
  4.5 13.0 %collective-permute-start = (f32[2,128,256]{2,1,0:T(8,128)S(1)}, f32[2,128,256]{2,1,0:T(8,128)S(1)}, u32[]{:S(2)}, u32[]{:S(2)}) collective-permute-start(f32[2,128,256]{2,1,0:T(8,128)S(1)} %get-tuple-element.27), channel_id=1, source_target_pairs={{8,0},{16,8},{24,16},{32,24},{40,32},{48,40},{56,48},{64,56},{72,6... | collective-permute-start | bytes 786440 | tf_op jit(solution)/shard_map/ppermute | solution.py:456
  8.7 12.4 %collective-permute-start.4 = (f32[2,128,256]{2,1,0:T(8,128)S(1)}, f32[2,128,256]{2,1,0:T(8,128)S(1)}, u32[]{:S(2)}, u32[]{:S(2)}) collective-permute-start(f32[2,128,256]{2,1,0:T(8,128)S(1)} %get-tuple-element.28), channel_id=1, source_target_pairs={{8,0},{16,8},{24,16},{32,24},{40,32},{48,40},{56,48},{64,56},{72,6... | collective-permute-start | bytes 786440 | tf_op jit(solution)/shard_map/ppermute | solution.py:456
  12.2 0.7 copy-start.1
  14.7 16.1 %collective-permute-start.11 = (f32[2,256,256]{2,1,0:T(8,128)S(1)}, f32[2,256,256]{2,1,0:T(8,128)S(1)}, u32[]{:S(2)}, u32[]{:S(2)}) collective-permute-start(f32[2,256,256]{2,1,0:T(8,128)S(1)} %pad_maximum_fusion), channel_id=1, source_target_pairs={{0,6},{1,3},{2,4},{3,1},{4,2},{5,7},{6,0},{7,5},{8,14},{9,11},{10,... | collective-permute-start | bytes 1572872 | tf_op jit(solution)/shard_map/ppermute | solution.py:451
  17.0 8.1 %collective-permute-start.8 = (f32[256,256]{1,0:T(8,128)S(1)}, f32[256,256]{1,0:T(8,128)S(1)}, u32[]{:S(2)}, u32[]{:S(2)}) collective-permute-start(f32[256,256]{1,0:T(8,128)S(1)} %get-tuple-element.54.mine_1), channel_id=1, source_target_pairs={{0,1},{1,0},{2,3},{3,2},{4,5},{5,4},{6,7},{7,6},{8,9},{9,8},{10,11... | collective-permute-start | bytes 786440 | tf_op jit(solution)/shard_map/ppermute | solution.py:443
  17.0 8.6 %collective-permute-start.10 = (f32[256,256]{1,0:T(8,128)S(1)}, f32[256,256]{1,0:T(8,128)S(1)}, u32[]{:S(2)}, u32[]{:S(2)}) collective-permute-start(f32[256,256]{1,0:T(8,128)S(1)} %tied.1.got_a), channel_id=1, source_target_pairs={{0,1},{1,0},{2,3},{3,2},{4,5},{5,4},{6,7},{7,6},{8,9},{9,8},{10,11... | collective-permute-start | bytes 786440 | tf_op jit(solution)/shard_map/ppermute | solution.py:443
  17.5 8.8 %collective-permute-start.1 = (f32[2,128,256]{2,1,0:T(8,128)S(1)}, f32[2,128,256]{2,1,0:T(8,128)S(1)}, u32[]{:S(2)}, u32[]{:S(2)}) collective-permute-start(f32[2,128,256]{2,1,0:T(8,128)S(1)} %collective-permute-done.refs_0_.h00), channel_id=1, source_target_pairs={{0,2},{1,7},{2,0},{3,5},{4,6},{5,3},{6,4},{7,1},{8,10},{9,15},{10,... | collective-permute-start | bytes 786440 | tf_op jit(solution)/shard_map/ppermute | solution.py:451
  21.1 8.1 %collective-permute-start.5 = (f32[2,128,256]{2,1,0:T(8,128)S(1)}, f32[2,128,256]{2,1,0:T(8,128)}, u32[]{:S(2)}, u32[]{:S(2)}) collective-permute-start(f32[2,128,256]{2,1,0:T(8,128)S(1)} %collective-permute-done.4.refs_4_.h10), channel_id=1, source_target_pairs={{0,2},{1,7},{2,0},{3,5},{4,6},{5,3},{6,4},{7,1},{8,10},{9,15},{10,... | collective-permute-start | bytes 786440 | tf_op jit(solution)/shard_map/ppermute | solution.py:451
  21.3 9.5 %all-to-all-start = ((s32[8,1,128]{2,1,0:T(1,128)}), s32[8,1,128]{2,1,0:T(1,128)S(1)}, u32[]{:S(2)}, u32[]{:S(2)}) async-start(s32[8,1,128]{2,1,0:T(1,128)} %row.1.refs_1_), calls=%async_computation | async-start | bytes 8192 | tf_op jit(solution)/shard_map/all_to_all | solution.py:504
  25.1 7.2 %collective-permute-start.2 = (f32[2,128,256]{2,1,0:T(8,128)S(1)}, f32[2,128,256]{2,1,0:T(8,128)}, u32[]{:S(2)}, u32[]{:S(2)}) collective-permute-start(f32[2,128,256]{2,1,0:T(8,128)S(1)} %collective-permute-done.refs_0_.h00), channel_id=1, source_target_pairs={{0,1},{1,0},{2,3},{3,2},{4,5},{5,4},{6,7},{7,6},{8,9},{9,8},{10,11... | collective-permute-start | bytes 786440 | tf_op jit(solution)/shard_map/ppermute | solution.py:443
  25.6 6.7 %collective-permute-start.6 = (f32[2,128,256]{2,1,0:T(8,128)S(1)}, f32[2,128,256]{2,1,0:T(8,128)}, u32[]{:S(2)}, u32[]{:S(2)}) collective-permute-start(f32[2,128,256]{2,1,0:T(8,128)S(1)} %collective-permute-done.4.refs_4_.h10), channel_id=1, source_target_pairs={{0,1},{1,0},{2,3},{3,2},{4,5},{5,4},{6,7},{7,6},{8,9},{9,8},{10,11... | collective-permute-start | bytes 786440 | tf_op jit(solution)/shard_map/ppermute | solution.py:443
  26.3 6.1 %collective-permute-start.3 = (f32[2,128,256]{2,1,0:T(8,128)S(1)}, f32[2,128,256]{2,1,0:T(8,128)}, u32[]{:S(2)}, u32[]{:S(2)}) collective-permute-start(f32[2,128,256]{2,1,0:T(8,128)S(1)} %collective-permute-done.1.refs_1_.h01), channel_id=1, source_target_pairs={{0,1},{1,0},{2,3},{3,2},{4,5},{5,4},{6,7},{7,6},{8,9},{9,8},{10,11... | collective-permute-start | bytes 786440 | tf_op jit(solution)/shard_map/ppermute | solution.py:443
  29.2 3.4 %collective-permute-start.7 = (f32[2,128,256]{2,1,0:T(8,128)}, f32[2,128,256]{2,1,0:T(8,128)}, u32[]{:S(2)}, u32[]{:S(2)}) collective-permute-start(f32[2,128,256]{2,1,0:T(8,128)} %collective-permute-done.5.refs_5_.h11), channel_id=1, source_target_pairs={{0,1},{1,0},{2,3},{3,2},{4,5},{5,4},{6,7},{7,6},{8,9},{9,8},{10,11... | collective-permute-start | bytes 786440 | tf_op jit(solution)/shard_map/ppermute | solution.py:443
  30.8 1.9 %collective-permute-start.12 = (f32[2,256,256]{2,1,0:T(8,128)S(1)}, f32[2,256,256]{2,1,0:T(8,128)S(1)}, u32[]{:S(2)}, u32[]{:S(2)}) collective-permute-start(f32[2,256,256]{2,1,0:T(8,128)S(1)} %collective-permute-done.11.got_b), channel_id=1, source_target_pairs={{0,1},{1,0},{2,3},{3,2},{4,5},{5,4},{6,7},{7,6},{8,9},{9,8},{10,11... | collective-permute-start | bytes 1572872 | tf_op jit(solution)/shard_map/ppermute | solution.py:443
  32.3 2.2 %copy-start = (f32[2,2,512,512]{3,2,1,0:T(8,128)S(1)}, f32[2,2,512,512]{3,2,1,0:T(8,128)}, u32[]{:S(2)}) copy-start(f32[2,2,512,512]{3,2,1,0:T(8,128)} %strip.1) | copy-start | bytes 12582916
  32.3 2.5 %copy-start.2 = (f32[2,2,256,256]{3,2,1,0:T(8,128)S(1)}, f32[2,2,256,256]{3,2,1,0:T(8,128)}, u32[]{:S(2)}) copy-start(f32[2,2,256,256]{3,2,1,0:T(8,128)} %probe.1) | copy-start | bytes 3145732
  32.3 2.8 %copy-start.3 = (bf16[9,256,256]{2,1,0:T(8,128)(2,1)S(1)}, bf16[9,256,256]{2,1,0:T(8,128)(2,1)}, u32[]{:S(2)}) copy-start(bf16[9,256,256]{2,1,0:T(8,128)(2,1)} %constant.27.clone.tables) | copy-start | bytes 3538948
  32.3 2.9 %copy-start.4 = (f32[2,256,256]{2,1,0:T(8,128)S(1)}, f32[2,256,256]{2,1,0:T(8,128)}, u32[]{:S(2)}) copy-start(f32[2,256,256]{2,1,0:T(8,128)} %constant.28.clone.transfer) | copy-start | bytes 1572868
  43.0 3.7 %collective-permute-start.13 = (f32[2,2,256,256]{3,2,1,0:T(8,128)S(1)}, f32[2,2,256,256]{3,2,1,0:T(8,128)S(1)}, u32[]{:S(2)}, u32[]{:S(2)}) collective-permute-start(f32[2,2,256,256]{3,2,1,0:T(8,128)S(1)} %get-tuple-element.30.g0), channel_id=1, source_target_pairs={{0,1},{1,0},{2,3},{3,2},{4,5},{5,4},{6,7},{7,6},{8,9},{9,8},{10,11... | collective-permute-start | bytes 3145736 | tf_op jit(solution)/shard_map/ppermute | solution.py:443
  43.5 3.0 %collective-permute-start.14 = (f32[2,256,256]{2,1,0:T(8,128)S(1)}, f32[2,256,256]{2,1,0:T(8,128)S(1)}, u32[]{:S(2)}, u32[]{:S(2)}) collective-permute-start(f32[2,256,256]{2,1,0:T(8,128)S(1)} %get-tuple-element.32), channel_id=1, source_target_pairs={{0,1},{1,0},{2,3},{3,2},{4,5},{5,4},{6,7},{7,6},{8,9},{9,8},{10,11... | collective-permute-start | bytes 1572872 | tf_op jit(solution)/shard_map/ppermute | solution.py:443
  48.7 31.7 %collective-permute-start.15 = (f32[2,2,4,64,256]{4,3,2,1,0:T(8,128)}, f32[2,2,4,64,256]{4,3,2,1,0:T(8,128)S(1)}, u32[]{:S(2)}, u32[]{:S(2)}) collective-permute-start(f32[2,2,4,64,256]{4,3,2,1,0:T(8,128)} %get-tuple-element.35), channel_id=1, source_target_pairs={{0,2},{1,7},{2,0},{3,5},{4,6},{5,3},{6,4},{7,1},{8,10},{9,15},{10,... | collective-permute-start | bytes 3145736 | tf_op jit(solution)/shard_map/ppermute | solution.py:451
  71.4 18.4 %all-to-all-start.2 = ((f32[8,32,256]{2,1,0:T(8,128)}), f32[8,32,256]{2,1,0:T(8,128)S(1)}, u32[]{:S(2)}, u32[]{:S(2)}) async-start(f32[8,32,256]{2,1,0:T(8,128)} %get-tuple-element.45), calls=%async_computation.2 | async-start | bytes 524288 | tf_op jit(solution)/shard_map/all_to_all | solution.py:546
  81.9 7.7 %collective-permute-start.17 = (f32[4,64,256]{2,1,0:T(8,128)S(1)}, f32[4,64,256]{2,1,0:T(8,128)S(1)}, u32[]{:S(2)}, u32[]{:S(2)}) collective-permute-start(f32[4,64,256]{2,1,0:T(8,128)S(1)} %get-tuple-element.42), channel_id=1, source_target_pairs={{0,6},{1,3},{2,4},{3,1},{4,2},{5,7},{6,0},{7,5},{8,14},{9,11},{10,... | collective-permute-start | bytes 786440 | tf_op jit(solution)/shard_map/ppermute | solution.py:451
  90.6 21.6 %all-to-all-start.3 = ((f32[16,32,256]{2,1,0:T(8,128)}), f32[16,32,256]{2,1,0:T(8,128)S(1)}, u32[]{:S(2)}, u32[]{:S(2)}) async-start(f32[16,32,256]{2,1,0:T(8,128)} %get-tuple-element.47), calls=%async_computation.3 | async-start | bytes 1048576 | tf_op jit(solution)/shard_map/all_to_all | solution.py:557
  96.4 15.7 %collective-permute-start.16 = (f32[4,64,512]{2,1,0:T(8,128)S(1)}, f32[4,64,512]{2,1,0:T(8,128)S(1)}, u32[]{:S(2)}, u32[]{:S(2)}) collective-permute-start(f32[4,64,512]{2,1,0:T(8,128)S(1)} %get-tuple-element.40), channel_id=1, source_target_pairs={{0,6},{1,3},{2,4},{3,1},{4,2},{5,7},{6,0},{7,5},{8,14},{9,11},{10,... | collective-permute-start | bytes 1572872 | tf_op jit(solution)/shard_map/ppermute | solution.py:451
  99.6 12.7 %collective-permute-start.18 = (f32[4,64,256]{2,1,0:T(8,128)S(1)}, f32[4,64,256]{2,1,0:T(8,128)S(1)}, u32[]{:S(2)}, u32[]{:S(2)}) collective-permute-start(f32[4,64,256]{2,1,0:T(8,128)S(1)} %get-tuple-element.44), channel_id=1, source_target_pairs={{0,8},{8,16},{16,24},{24,32},{32,40},{40,48},{48,56},{56,64},{64,7... | collective-permute-start | bytes 786440 | tf_op jit(solution)/shard_map/ppermute | solution.py:456
  112.2 1.9 %collective-permute-start.19 = (f32[2,256,256]{2,1,0:T(8,128)S(1)}, f32[2,256,256]{2,1,0:T(8,128)S(1)}, u32[]{:S(2)}, u32[]{:S(2)}) collective-permute-start(f32[2,256,256]{2,1,0:T(8,128)S(1)} %bitcast.17), channel_id=1, source_target_pairs={{0,1},{1,0},{2,3},{3,2},{4,5},{5,4},{6,7},{7,6},{8,9},{9,8},{10,11... | collective-permute-start | bytes 1572872 | tf_op jit(solution)/shard_map/ppermute | solution.py:443

commit v4 on v3

--- a/solution.py
+++ b/solution.py
@@ -389,7 +389,9 @@
     token[...] = before[...]
 
 
-def stack_kernel(core, x, y, out):
+def last_kernel(core, x, y, keep, got, edge, out, rows):
+    rows[:, :, :256] = keep[:, :, :256] + got[:, :, :256] + edge[...]
+    rows[:, :, 256:] = keep[:, :, 256:] + got[:, :, 256:]
     for part in range(2):
         out[part, core[0]] = x[part]
         out[part, 1 - core[0]] = y[part]
@@ -555,12 +557,11 @@
     edge = tile_shift(edge, 1)
     spread_2, token = spread(pieces_2, 16, 1.0 / 16.0, token)
     total = lax.all_to_all(spread_2, ("x", "y"), 0, 0, tiled=True).reshape(2, n, n)
-    strip = keep_strip + got_strip
-    rows = jnp.concatenate([strip[:, :, :n] + edge, strip[:, :, n:]], 2)
     other = core_swap(total)
-    probe_gradient = run_kernel(
-        stack_kernel, "stacked", (c[None], total, other), [SMEM, VMEM, VMEM],
-        struct(2, 2, n, n), VMEM, [], LONG, 4,
+    probe_gradient, rows = run_kernel(
+        last_kernel, "last", (c[None], total, other, keep_strip, got_strip, edge),
+        [SMEM] + [VMEM] * 5, [struct(2, 2, n, n), struct(4, 64, 512)], [VMEM] * 2,
+        [], 1 << 20, 4,
     )
     return rows.reshape(2, 2, 64, 512), probe_gradient
 

time: 116 us -> 121 us (1.043)
  waiting for transfers between devices: 25.3 us -> 33 us
  starting transfers between devices: 42.7 us -> 41.1 us
    ppermute x3, waiting for transfers between devices: 2.96 us -> 11.8 us  [tile_shift(): lax.ppermute(x, ('z', 'x'), [(i, i + by) for i in range(n) if 0 <= i + by...]
    all_to_all x1, waiting for transfers between devices: 9.21 us -> 7.01 us  [shards(): lax.all_to_all(spread_2, ('x', 'y'), 0, 0, tiled=True).reshape(2, n, n)]
    ppermute x7, waiting for transfers between devices: 8.78 us -> 10.6 us  [y_swap(): return lax.ppermute(x, ('y', 'c'), pairs(8, partner))]
    ppermute x3, starting transfers between devices: 10.3 us -> 8.85 us  [tile_shift(): lax.ppermute(x, ('z', 'x'), [(i, i + by) for i in range(n) if 0 <= i + by...]
  transfers between devices with their start and end apart: 23 -> 23, of which waited for: 10 -> 11; matrix products, arithmetic and copies ran while one was open for 1% -> 0% of each run, Pallas kernels for 5% -> 5%
where the time goes in v4:
time: 121 us
  starting transfers between devices  41.1 us (34%)
  waiting for transfers between devices  33 us (27%)
  blocking collectives  21.9 us (18%)
  Pallas kernels  17.5 us (14%)
  local copies, waits for them, and re-layouts  5.41 us (4%)
  between operations  1.45 us (1%)
    all_to_all x1, blocking collectives, shards(): lax.all_to_all(total.reshape(16, 32, n), ('x', 'y'), 0, 0, tiled=True)  21.9 us
    pallas_call x11, Pallas kernels, run_kernel(): pl.pallas_call(body, out_shape=outs, in_specs=in_specs, out_specs=out_spe...  16.8 us
    ppermute x3, waiting for transfers between devices, tile_shift(): lax.ppermute(x, ('z', 'x'), [(i, i + by) for i in range(n) if 0 <= i + by...  11.8 us
    ppermute x7, waiting for transfers between devices, y_swap(): return lax.ppermute(x, ('y', 'c'), pairs(8, partner))  10.6 us
    ppermute x7, starting transfers between devices, y_swap(): return lax.ppermute(x, ('y', 'c'), pairs(8, partner))  9.51 us
    all_to_all x1, starting transfers between devices, shards(): pieces_2 = lax.all_to_all(spread_1, 'z', 0, 0, tiled=True)  8.98 us
    ppermute x3, starting transfers between devices, tile_shift(): lax.ppermute(x, ('z', 'x'), [(i, i + by) for i in range(n) if 0 <= i + by...  8.85 us
    all_to_all x1, waiting for transfers between devices, shards(): lax.all_to_all(spread_2, ('x', 'y'), 0, 0, tiled=True).reshape(2, n, n)  7.01 us
  transfers between devices with their start and end apart: 23, of which 11 were waited for; matrix products, arithmetic and copies ran while one was open for 0% of the time, Pallas kernels for 5%

profile of v4, /device:TPU:32, one launch (start us, length us, event | category | flops | bytes accessed | tf_op | source)
XLA Modules:
  0.0 120.6 jit_solution(5917651382506492477)
XLA Ops:
  0.6 1.1 dynamic-slice_bitcast_fusion
  1.7 1.1 slice_bitcast_fusion
  2.8 1.7 %collective-permute-start.9 = (f32[256,256]{1,0:T(8,128)S(1)}, f32[256,256]{1,0:T(8,128)S(1)}, u32[]{:S(2)}, u32[]{:S(2)}) collective-permute-start(f32[256,256]{1,0:T(8,128)S(1)} %get-tuple-element.56.mine_1), channel_id=1, source_target_pairs={{0,2},{1,7},{2,0},{3,5},{4,6},{5,3},{6,4},{7,1},{8,10},{9,15},{10,... | collective-permute-start | bytes 786440 | tf_op jit(solution)/shard_map/ppermute | solution.py:453
  4.5 4.2 %collective-permute-start = (f32[2,128,256]{2,1,0:T(8,128)S(1)}, f32[2,128,256]{2,1,0:T(8,128)S(1)}, u32[]{:S(2)}, u32[]{:S(2)}) collective-permute-start(f32[2,128,256]{2,1,0:T(8,128)S(1)} %get-tuple-element.29), channel_id=1, source_target_pairs={{8,0},{16,8},{24,16},{32,24},{40,32},{48,40},{56,48},{64,56},{72,6... | collective-permute-start | bytes 786440 | tf_op jit(solution)/shard_map/ppermute | solution.py:458
  8.7 2.7 %collective-permute-start.4 = (f32[2,128,256]{2,1,0:T(8,128)S(1)}, f32[2,128,256]{2,1,0:T(8,128)S(1)}, u32[]{:S(2)}, u32[]{:S(2)}) collective-permute-start(f32[2,128,256]{2,1,0:T(8,128)S(1)} %get-tuple-element.30), channel_id=1, source_target_pairs={{8,0},{16,8},{24,16},{32,24},{40,32},{48,40},{56,48},{64,56},{72,6... | collective-permute-start | bytes 786440 | tf_op jit(solution)/shard_map/ppermute | solution.py:458
  12.8 1.2 row.1.refs_1_
  14.0 0.7 tied.1.got_a
  14.7 2.3 %collective-permute-start.11 = (f32[2,256,256]{2,1,0:T(8,128)S(1)}, f32[2,256,256]{2,1,0:T(8,128)S(1)}, u32[]{:S(2)}, u32[]{:S(2)}) collective-permute-start(f32[2,256,256]{2,1,0:T(8,128)S(1)} %pad_maximum_fusion), channel_id=1, source_target_pairs={{0,6},{1,3},{2,4},{3,1},{4,2},{5,7},{6,0},{7,5},{8,14},{9,11},{10,... | collective-permute-start | bytes 1572872 | tf_op jit(solution)/shard_map/ppermute | solution.py:453
  18.2 3.0 %collective-permute-done.4.refs_4_.h10 = f32[2,128,256]{2,1,0:T(8,128)S(1)} collective-permute-done((f32[2,128,256]{2,1,0:T(8,128)S(1)}, f32[2,128,256]{2,1,0:T(8,128)S(1)}, u32[]{:S(2)}, u32[]{:S(2)}) %collective-permute-start.4) | collective-permute-done | bytes 262176 | tf_op jit(solution)/shard_map/ppermute | solution.py:458
  21.3 3.8 %all-to-all-start = ((s32[8,1,128]{2,1,0:T(1,128)}), s32[8,1,128]{2,1,0:T(1,128)S(1)}, u32[]{:S(2)}, u32[]{:S(2)}) async-start(s32[8,1,128]{2,1,0:T(1,128)} %row.1.refs_1_), calls=%async_computation | async-start | bytes 8192 | tf_op jit(solution)/shard_map/all_to_all | solution.py:506
  26.3 0.8 collective-permute-start.3
  27.1 2.1 %collective-permute-done.5.refs_5_.h11 = f32[2,128,256]{2,1,0:T(8,128)} collective-permute-done((f32[2,128,256]{2,1,0:T(8,128)S(1)}, f32[2,128,256]{2,1,0:T(8,128)}, u32[]{:S(2)}, u32[]{:S(2)}) %collective-permute-start.5) | collective-permute-done | bytes 262176 | tf_op jit(solution)/shard_map/ppermute | solution.py:453
  29.2 1.6 %collective-permute-start.7 = (f32[2,128,256]{2,1,0:T(8,128)}, f32[2,128,256]{2,1,0:T(8,128)}, u32[]{:S(2)}, u32[]{:S(2)}) collective-permute-start(f32[2,128,256]{2,1,0:T(8,128)} %collective-permute-done.5.refs_5_.h11), channel_id=1, source_target_pairs={{0,1},{1,0},{2,3},{3,2},{4,5},{5,4},{6,7},{7,6},{8,9},{9,8},{10,11... | collective-permute-start | bytes 786440 | tf_op jit(solution)/shard_map/ppermute | solution.py:445
  30.8 1.4 %plan.1 = s32[9,4]{1,0:T(8,128)S(1)} custom-call(s32[8,1,128]{2,1,0:T(1,128)S(1)} %all-to-all-done.info, s32[2]{0:T(128)S(1)} %pad_add_fusion.place.me), custom_call_target="tpu_custom_call" | custom-call | flops 8589934592 | bytes 262144 | tf_op jit(solution)/shard_map/plan/pallas_call | solution.py:416
  32.7 1.8 %copy-done = f32[2,2,512,512]{3,2,1,0:T(8,128)S(1)} copy-done((f32[2,2,512,512]{3,2,1,0:T(8,128)S(1)}, f32[2,2,512,512]{3,2,1,0:T(8,128)}, u32[]{:S(2)}) %copy-start) | copy-done | bytes 4194328
  35.2 7.8 %position.1 = (f32[2,2,256,256]{3,2,1,0:T(8,128)S(1)}, f32[2,256,256]{2,1,0:T(8,128)S(1)}, f32[2,256,256]{2,1,0:T(8,128)S(1)}) custom-call(s32[9,4]{1,0:T(8,128)S(1)} %plan.1, f32[8,128]{1,0:T(8,128)S(1)} %joined.1, f32[2,2,512,512]{3,2,1,0:T(8,128)S(1)} %copy-done, f32[2,128,256]{2,1,0:T(8,128)S(1)} %collective-permute-done.refs_0_.h00, ...), custom_call_target="tpu_custom_call" | custom-call | flops 4831838208 | bytes 16777216 | tf_op jit(solution)/shard_map/position/pallas_call | solution.py:416
  43.7 2.9 %collective-permute-done.13.y = f32[2,256,256]{2,1,0:T(8,128)S(1)} collective-permute-done((f32[2,256,256]{2,1,0:T(8,128)S(1)}, f32[2,256,256]{2,1,0:T(8,128)S(1)}, u32[]{:S(2)}, u32[]{:S(2)}) %collective-permute-start.13) | collective-permute-done | bytes 524320 | tf_op jit(solution)/shard_map/ppermute | solution.py:445
  46.7 2.0 %rows.1 = (f32[2,2,4,64,256]{4,3,2,1,0:T(8,128)}, f32[2,2,4,64,256]{4,3,2,1,0:T(8,128)S(1)}, f32[8,128]{1,0:T(8,128)S(1)}) custom-call(s32[9,4]{1,0:T(8,128)S(1)} %plan.1, f32[2,2,256,256]{3,2,1,0:T(8,128)S(1)} %get-tuple-element.35.g0, f32[2,2,256,256]{3,2,1,0:T(8,128)S(1)} %collective-permute-done.14.g1, f32[8,128]{1,0:T(8,128)S(1)} %get-tuple-element.36.before), custom_call_target="tpu_custom_call" | custom-call | flops 1048576 | bytes 262144 | tf_op jit(solution)/shard_map/rows/pallas_call | solution.py:416
  48.7 21.9 %all_to_all.20.refs_0_ = f32[16,32,256]{2,1,0:T(8,128)S(1)} all-to-all(f32[16,32,256]{2,1,0:T(8,128)S(1)} %bitcast.19), channel_id=1, replica_groups=mesh['z'=8,'x'=4,'y'=4,'c'=2] {'x','y'}, dimensions={0} | all-to-all | bytes 1048576 | tf_op jit(solution)/shard_map/all_to_all | solution.py:540
  70.7 0.7 spread.2
  71.4 9.0 %all-to-all-start.2 = ((f32[8,32,256]{2,1,0:T(8,128)}), f32[8,32,256]{2,1,0:T(8,128)S(1)}, u32[]{:S(2)}, u32[]{:S(2)}) async-start(f32[8,32,256]{2,1,0:T(8,128)} %get-tuple-element.38), calls=%async_computation.2 | async-start | bytes 524288 | tf_op jit(solution)/shard_map/all_to_all | solution.py:548
  80.4 1.4 %place.1 = (f32[4,64,256]{2,1,0:T(8,128)S(1)}, f32[4,64,512]{2,1,0:T(8,128)S(1)}, f32[4,64,256]{2,1,0:T(8,128)S(1)}, f32[4,64,512]{2,1,0:T(8,128)S(1)}, f32[8,128]{1,0:T(8,128)S(1)}) custom-call(s32[9,4]{1,0:T(8,128)S(1)} %plan.1, f32[2,2,4,64,256]{4,3,2,1,0:T(8,128)S(1)} %get-tuple-element.39.kept, f32[2,2,4,64,256]{4,3,2,1,0:T(8,128)S(1)} %collective-permute-done.15.got, ...), custom_call_target="tpu_custom_call" | custom-call | flops 1048576 | bytes 262144 | tf_op jit(solution)/shard_map/place/pallas_call | solution.py:416
  81.8 1.6 %collective-permute-start.16 = (f32[4,64,256]{2,1,0:T(8,128)S(1)}, f32[4,64,256]{2,1,0:T(8,128)S(1)}, u32[]{:S(2)}, u32[]{:S(2)}) collective-permute-start(f32[4,64,256]{2,1,0:T(8,128)S(1)} %get-tuple-element.43), channel_id=1, source_target_pairs={{0,6},{1,3},{2,4},{3,1},{4,2},{5,7},{6,0},{7,5},{8,14},{9,11},{10,... | collective-permute-start | bytes 786440 | tf_op jit(solution)/shard_map/ppermute | solution.py:453
  83.4 6.1 %collective-permute-done.16.y = f32[4,64,256]{2,1,0:T(8,128)S(1)} collective-permute-done((f32[4,64,256]{2,1,0:T(8,128)S(1)}, f32[4,64,256]{2,1,0:T(8,128)S(1)}, u32[]{:S(2)}, u32[]{:S(2)}) %collective-permute-start.16) | collective-permute-done | bytes 262176 | tf_op jit(solution)/shard_map/ppermute | solution.py:453
  89.8 0.9 spread.3
  90.6 5.8 %all-to-all-start.3 = ((f32[16,32,256]{2,1,0:T(8,128)}), f32[16,32,256]{2,1,0:T(8,128)S(1)}, u32[]{:S(2)}, u32[]{:S(2)}) async-start(f32[16,32,256]{2,1,0:T(8,128)} %get-tuple-element.46), calls=%async_computation.3 | async-start | bytes 1048576 | tf_op jit(solution)/shard_map/all_to_all | solution.py:559
  96.4 3.1 %collective-permute-start.18 = (f32[4,64,512]{2,1,0:T(8,128)S(1)}, f32[4,64,512]{2,1,0:T(8,128)S(1)}, u32[]{:S(2)}, u32[]{:S(2)}) collective-permute-start(f32[4,64,512]{2,1,0:T(8,128)S(1)} %get-tuple-element.48), channel_id=1, source_target_pairs={{0,6},{1,3},{2,4},{3,1},{4,2},{5,7},{6,0},{7,5},{8,14},{9,11},{10,... | collective-permute-start | bytes 1572872 | tf_op jit(solution)/shard_map/ppermute | solution.py:453
  99.6 7.0 %all-to-all-done.3 = f32[16,32,256]{2,1,0:T(8,128)S(1)} async-done(((f32[16,32,256]{2,1,0:T(8,128)}), f32[16,32,256]{2,1,0:T(8,128)S(1)}, u32[]{:S(2)}, u32[]{:S(2)}) %all-to-all-start.3) | async-done | bytes 524320 | tf_op jit(solution)/shard_map/all_to_all | solution.py:559
  106.6 1.9 %collective-permute-start.19 = (f32[4,64,256]{2,1,0:T(8,128)S(1)}, f32[4,64,256]{2,1,0:T(8,128)S(1)}, u32[]{:S(2)}, u32[]{:S(2)}) collective-permute-start(f32[4,64,256]{2,1,0:T(8,128)S(1)} %get-tuple-element.49), channel_id=1, source_target_pairs={{0,8},{8,16},{16,24},{24,32},{32,40},{40,48},{48,56},{56,64},{64,7... | collective-permute-start | bytes 786440 | tf_op jit(solution)/shard_map/ppermute | solution.py:458
  108.5 1.9 %collective-permute-done.18.got = f32[4,64,512]{2,1,0:T(8,128)S(1)} collective-permute-done((f32[4,64,512]{2,1,0:T(8,128)S(1)}, f32[4,64,512]{2,1,0:T(8,128)S(1)}, u32[]{:S(2)}, u32[]{:S(2)}) %collective-permute-start.18) | collective-permute-done | bytes 524320 | tf_op jit(solution)/shard_map/ppermute | solution.py:453
  110.4 8.9 %collective-permute-done.19.edge = f32[4,64,256]{2,1,0:T(8,128)S(1)} collective-permute-done((f32[4,64,256]{2,1,0:T(8,128)S(1)}, f32[4,64,256]{2,1,0:T(8,128)S(1)}, u32[]{:S(2)}, u32[]{:S(2)}) %collective-permute-start.19) | collective-permute-done | bytes 262176 | tf_op jit(solution)/shard_map/ppermute | solution.py:458
  119.3 1.3 %last.1 = (f32[2,2,256,256]{3,2,1,0:T(8,128)}, f32[4,64,512]{2,1,0:T(8,128)}) custom-call(s32[1]{0:T(128)} %bitcast.core, f32[2,256,256]{2,1,0:T(8,128)S(1)} %bitcast.17, f32[2,256,256]{2,1,0:T(8,128)S(1)} %collective-permute-done.17.y, f32[4,64,512]{2,1,0:T(8,128)S(1)} %get-tuple-element.47.keep, f32[4,64,512]{2,1,0:T(8,128)S(1)} %collective-permute-done.18.got, ...), custom_call_target="tpu_custom_call" | custom-call | flops 1048576 | bytes 262144 | tf_op jit(solution)/shard_map/last/pallas_call | solution.py:416
  (42 shorter events, 5.5 us)
Async XLA Ops:
  2.8 11.2 %collective-permute-start.9 = (f32[256,256]{1,0:T(8,128)S(1)}, f32[256,256]{1,0:T(8,128)S(1)}, u32[]{:S(2)}, u32[]{:S(2)}) collective-permute-start(f32[256,256]{1,0:T(8,128)S(1)} %get-tuple-element.56.mine_1), channel_id=1, source_target_pairs={{0,2},{1,7},{2,0},{3,5},{4,6},{5,3},{6,4},{7,1},{8,10},{9,15},{10,... | collective-permute-start | bytes 786440 | tf_op jit(solution)/shard_map/ppermute | solution.py:453
  4.5 13.0 %collective-permute-start = (f32[2,128,256]{2,1,0:T(8,128)S(1)}, f32[2,128,256]{2,1,0:T(8,128)S(1)}, u32[]{:S(2)}, u32[]{:S(2)}) collective-permute-start(f32[2,128,256]{2,1,0:T(8,128)S(1)} %get-tuple-element.29), channel_id=1, source_target_pairs={{8,0},{16,8},{24,16},{32,24},{40,32},{48,40},{56,48},{64,56},{72,6... | collective-permute-start | bytes 786440 | tf_op jit(solution)/shard_map/ppermute | solution.py:458
  8.7 12.4 %collective-permute-start.4 = (f32[2,128,256]{2,1,0:T(8,128)S(1)}, f32[2,128,256]{2,1,0:T(8,128)S(1)}, u32[]{:S(2)}, u32[]{:S(2)}) collective-permute-start(f32[2,128,256]{2,1,0:T(8,128)S(1)} %get-tuple-element.30), channel_id=1, source_target_pairs={{8,0},{16,8},{24,16},{32,24},{40,32},{48,40},{56,48},{64,56},{72,6... | collective-permute-start | bytes 786440 | tf_op jit(solution)/shard_map/ppermute | solution.py:458
  12.2 0.7 copy-start.1
  14.7 16.1 %collective-permute-start.11 = (f32[2,256,256]{2,1,0:T(8,128)S(1)}, f32[2,256,256]{2,1,0:T(8,128)S(1)}, u32[]{:S(2)}, u32[]{:S(2)}) collective-permute-start(f32[2,256,256]{2,1,0:T(8,128)S(1)} %pad_maximum_fusion), channel_id=1, source_target_pairs={{0,6},{1,3},{2,4},{3,1},{4,2},{5,7},{6,0},{7,5},{8,14},{9,11},{10,... | collective-permute-start | bytes 1572872 | tf_op jit(solution)/shard_map/ppermute | solution.py:453
  17.0 8.1 %collective-permute-start.8 = (f32[256,256]{1,0:T(8,128)S(1)}, f32[256,256]{1,0:T(8,128)S(1)}, u32[]{:S(2)}, u32[]{:S(2)}) collective-permute-start(f32[256,256]{1,0:T(8,128)S(1)} %get-tuple-element.56.mine_1), channel_id=1, source_target_pairs={{0,1},{1,0},{2,3},{3,2},{4,5},{5,4},{6,7},{7,6},{8,9},{9,8},{10,11... | collective-permute-start | bytes 786440 | tf_op jit(solution)/shard_map/ppermute | solution.py:445
  17.0 8.6 %collective-permute-start.10 = (f32[256,256]{1,0:T(8,128)S(1)}, f32[256,256]{1,0:T(8,128)S(1)}, u32[]{:S(2)}, u32[]{:S(2)}) collective-permute-start(f32[256,256]{1,0:T(8,128)S(1)} %tied.1.got_a), channel_id=1, source_target_pairs={{0,1},{1,0},{2,3},{3,2},{4,5},{5,4},{6,7},{7,6},{8,9},{9,8},{10,11... | collective-permute-start | bytes 786440 | tf_op jit(solution)/shard_map/ppermute | solution.py:445
  17.5 8.8 %collective-permute-start.1 = (f32[2,128,256]{2,1,0:T(8,128)S(1)}, f32[2,128,256]{2,1,0:T(8,128)S(1)}, u32[]{:S(2)}, u32[]{:S(2)}) collective-permute-start(f32[2,128,256]{2,1,0:T(8,128)S(1)} %collective-permute-done.refs_0_.h00), channel_id=1, source_target_pairs={{0,2},{1,7},{2,0},{3,5},{4,6},{5,3},{6,4},{7,1},{8,10},{9,15},{10,... | collective-permute-start | bytes 786440 | tf_op jit(solution)/shard_map/ppermute | solution.py:453
  21.1 8.1 %collective-permute-start.5 = (f32[2,128,256]{2,1,0:T(8,128)S(1)}, f32[2,128,256]{2,1,0:T(8,128)}, u32[]{:S(2)}, u32[]{:S(2)}) collective-permute-start(f32[2,128,256]{2,1,0:T(8,128)S(1)} %collective-permute-done.4.refs_4_.h10), channel_id=1, source_target_pairs={{0,2},{1,7},{2,0},{3,5},{4,6},{5,3},{6,4},{7,1},{8,10},{9,15},{10,... | collective-permute-start | bytes 786440 | tf_op jit(solution)/shard_map/ppermute | solution.py:453
  21.3 9.5 %all-to-all-start = ((s32[8,1,128]{2,1,0:T(1,128)}), s32[8,1,128]{2,1,0:T(1,128)S(1)}, u32[]{:S(2)}, u32[]{:S(2)}) async-start(s32[8,1,128]{2,1,0:T(1,128)} %row.1.refs_1_), calls=%async_computation | async-start | bytes 8192 | tf_op jit(solution)/shard_map/all_to_all | solution.py:506
  25.1 7.2 %collective-permute-start.2 = (f32[2,128,256]{2,1,0:T(8,128)S(1)}, f32[2,128,256]{2,1,0:T(8,128)}, u32[]{:S(2)}, u32[]{:S(2)}) collective-permute-start(f32[2,128,256]{2,1,0:T(8,128)S(1)} %collective-permute-done.refs_0_.h00), channel_id=1, source_target_pairs={{0,1},{1,0},{2,3},{3,2},{4,5},{5,4},{6,7},{7,6},{8,9},{9,8},{10,11... | collective-permute-start | bytes 786440 | tf_op jit(solution)/shard_map/ppermute | solution.py:445
  25.6 6.7 %collective-permute-start.6 = (f32[2,128,256]{2,1,0:T(8,128)S(1)}, f32[2,128,256]{2,1,0:T(8,128)}, u32[]{:S(2)}, u32[]{:S(2)}) collective-permute-start(f32[2,128,256]{2,1,0:T(8,128)S(1)} %collective-permute-done.4.refs_4_.h10), channel_id=1, source_target_pairs={{0,1},{1,0},{2,3},{3,2},{4,5},{5,4},{6,7},{7,6},{8,9},{9,8},{10,11... | collective-permute-start | bytes 786440 | tf_op jit(solution)/shard_map/ppermute | solution.py:445
  26.3 6.1 %collective-permute-start.3 = (f32[2,128,256]{2,1,0:T(8,128)S(1)}, f32[2,128,256]{2,1,0:T(8,128)}, u32[]{:S(2)}, u32[]{:S(2)}) collective-permute-start(f32[2,128,256]{2,1,0:T(8,128)S(1)} %collective-permute-done.1.refs_1_.h01), channel_id=1, source_target_pairs={{0,1},{1,0},{2,3},{3,2},{4,5},{5,4},{6,7},{7,6},{8,9},{9,8},{10,11... | collective-permute-start | bytes 786440 | tf_op jit(solution)/shard_map/ppermute | solution.py:445
  29.2 3.4 %collective-permute-start.7 = (f32[2,128,256]{2,1,0:T(8,128)}, f32[2,128,256]{2,1,0:T(8,128)}, u32[]{:S(2)}, u32[]{:S(2)}) collective-permute-start(f32[2,128,256]{2,1,0:T(8,128)} %collective-permute-done.5.refs_5_.h11), channel_id=1, source_target_pairs={{0,1},{1,0},{2,3},{3,2},{4,5},{5,4},{6,7},{7,6},{8,9},{9,8},{10,11... | collective-permute-start | bytes 786440 | tf_op jit(solution)/shard_map/ppermute | solution.py:445
  30.8 1.9 %collective-permute-start.12 = (f32[2,256,256]{2,1,0:T(8,128)S(1)}, f32[2,256,256]{2,1,0:T(8,128)S(1)}, u32[]{:S(2)}, u32[]{:S(2)}) collective-permute-start(f32[2,256,256]{2,1,0:T(8,128)S(1)} %collective-permute-done.11.got_b), channel_id=1, source_target_pairs={{0,1},{1,0},{2,3},{3,2},{4,5},{5,4},{6,7},{7,6},{8,9},{9,8},{10,11... | collective-permute-start | bytes 1572872 | tf_op jit(solution)/shard_map/ppermute | solution.py:445
  32.3 2.2 %copy-start = (f32[2,2,512,512]{3,2,1,0:T(8,128)S(1)}, f32[2,2,512,512]{3,2,1,0:T(8,128)}, u32[]{:S(2)}) copy-start(f32[2,2,512,512]{3,2,1,0:T(8,128)} %strip.1) | copy-start | bytes 12582916
  32.3 2.5 %copy-start.2 = (f32[2,2,256,256]{3,2,1,0:T(8,128)S(1)}, f32[2,2,256,256]{3,2,1,0:T(8,128)}, u32[]{:S(2)}) copy-start(f32[2,2,256,256]{3,2,1,0:T(8,128)} %probe.1) | copy-start | bytes 3145732
  32.3 2.8 %copy-start.3 = (bf16[9,256,256]{2,1,0:T(8,128)(2,1)S(1)}, bf16[9,256,256]{2,1,0:T(8,128)(2,1)}, u32[]{:S(2)}) copy-start(bf16[9,256,256]{2,1,0:T(8,128)(2,1)} %constant.27.clone.tables) | copy-start | bytes 3538948
  32.3 2.9 %copy-start.4 = (f32[2,256,256]{2,1,0:T(8,128)S(1)}, f32[2,256,256]{2,1,0:T(8,128)}, u32[]{:S(2)}) copy-start(f32[2,256,256]{2,1,0:T(8,128)} %constant.28.clone.transfer) | copy-start | bytes 1572868
  43.0 3.7 %collective-permute-start.14 = (f32[2,2,256,256]{3,2,1,0:T(8,128)S(1)}, f32[2,2,256,256]{3,2,1,0:T(8,128)S(1)}, u32[]{:S(2)}, u32[]{:S(2)}) collective-permute-start(f32[2,2,256,256]{3,2,1,0:T(8,128)S(1)} %get-tuple-element.35.g0), channel_id=1, source_target_pairs={{0,1},{1,0},{2,3},{3,2},{4,5},{5,4},{6,7},{7,6},{8,9},{9,8},{10,11... | collective-permute-start | bytes 3145736 | tf_op jit(solution)/shard_map/ppermute | solution.py:445
  43.6 3.0 %collective-permute-start.13 = (f32[2,256,256]{2,1,0:T(8,128)S(1)}, f32[2,256,256]{2,1,0:T(8,128)S(1)}, u32[]{:S(2)}, u32[]{:S(2)}) collective-permute-start(f32[2,256,256]{2,1,0:T(8,128)S(1)} %get-tuple-element.33), channel_id=1, source_target_pairs={{0,1},{1,0},{2,3},{3,2},{4,5},{5,4},{6,7},{7,6},{8,9},{9,8},{10,11... | collective-permute-start | bytes 1572872 | tf_op jit(solution)/shard_map/ppermute | solution.py:445
  48.7 31.7 %collective-permute-start.15 = (f32[2,2,4,64,256]{4,3,2,1,0:T(8,128)}, f32[2,2,4,64,256]{4,3,2,1,0:T(8,128)S(1)}, u32[]{:S(2)}, u32[]{:S(2)}) collective-permute-start(f32[2,2,4,64,256]{4,3,2,1,0:T(8,128)} %get-tuple-element.40), channel_id=1, source_target_pairs={{0,2},{1,7},{2,0},{3,5},{4,6},{5,3},{6,4},{7,1},{8,10},{9,15},{10,... | collective-permute-start | bytes 3145736 | tf_op jit(solution)/shard_map/ppermute | solution.py:453
  71.4 18.4 %all-to-all-start.2 = ((f32[8,32,256]{2,1,0:T(8,128)}), f32[8,32,256]{2,1,0:T(8,128)S(1)}, u32[]{:S(2)}, u32[]{:S(2)}) async-start(f32[8,32,256]{2,1,0:T(8,128)} %get-tuple-element.38), calls=%async_computation.2 | async-start | bytes 524288 | tf_op jit(solution)/shard_map/all_to_all | solution.py:548
  81.8 7.7 %collective-permute-start.16 = (f32[4,64,256]{2,1,0:T(8,128)S(1)}, f32[4,64,256]{2,1,0:T(8,128)S(1)}, u32[]{:S(2)}, u32[]{:S(2)}) collective-permute-start(f32[4,64,256]{2,1,0:T(8,128)S(1)} %get-tuple-element.43), channel_id=1, source_target_pairs={{0,6},{1,3},{2,4},{3,1},{4,2},{5,7},{6,0},{7,5},{8,14},{9,11},{10,... | collective-permute-start | bytes 786440 | tf_op jit(solution)/shard_map/ppermute | solution.py:453
  90.6 15.9 %all-to-all-start.3 = ((f32[16,32,256]{2,1,0:T(8,128)}), f32[16,32,256]{2,1,0:T(8,128)S(1)}, u32[]{:S(2)}, u32[]{:S(2)}) async-start(f32[16,32,256]{2,1,0:T(8,128)} %get-tuple-element.46), calls=%async_computation.3 | async-start | bytes 1048576 | tf_op jit(solution)/shard_map/all_to_all | solution.py:559
  96.4 14.0 %collective-permute-start.18 = (f32[4,64,512]{2,1,0:T(8,128)S(1)}, f32[4,64,512]{2,1,0:T(8,128)S(1)}, u32[]{:S(2)}, u32[]{:S(2)}) collective-permute-start(f32[4,64,512]{2,1,0:T(8,128)S(1)} %get-tuple-element.48), channel_id=1, source_target_pairs={{0,6},{1,3},{2,4},{3,1},{4,2},{5,7},{6,0},{7,5},{8,14},{9,11},{10,... | collective-permute-start | bytes 1572872 | tf_op jit(solution)/shard_map/ppermute | solution.py:453
  106.6 12.7 %collective-permute-start.17 = (f32[2,256,256]{2,1,0:T(8,128)S(1)}, f32[2,256,256]{2,1,0:T(8,128)S(1)}, u32[]{:S(2)}, u32[]{:S(2)}) collective-permute-start(f32[2,256,256]{2,1,0:T(8,128)S(1)} %bitcast.16), channel_id=1, source_target_pairs={{0,1},{1,0},{2,3},{3,2},{4,5},{5,4},{6,7},{7,6},{8,9},{9,8},{10,11... | collective-permute-start | bytes 1572872 | tf_op jit(solution)/shard_map/ppermute | solution.py:445
  106.6 12.7 %collective-permute-start.19 = (f32[4,64,256]{2,1,0:T(8,128)S(1)}, f32[4,64,256]{2,1,0:T(8,128)S(1)}, u32[]{:S(2)}, u32[]{:S(2)}) collective-permute-start(f32[4,64,256]{2,1,0:T(8,128)S(1)} %get-tuple-element.49), channel_id=1, source_target_pairs={{0,8},{8,16},{16,24},{24,32},{32,40},{40,48},{48,56},{56,64},{64,7... | collective-permute-start | bytes 786440 | tf_op jit(solution)/shard_map/ppermute | solution.py:458
